TPU v7x, 128 devices: a whole 4x4x4 slice. The times are simulated.
128 devices in a mesh: seq: 32 (over y, z, core), head: 4 (over x).
Axes of the slice: x: 4, y: 4, z: 4, core: 2. Of those that a mesh axis runs over, the one named last changes fastest.
Arguments:
- queries: bfloat16 [12288, 2560], P('seq', 'head'), may hold values from -24 to 24
- keys: bfloat16 [12288, 2560], P('seq', 'head'), may hold values from -8 to 8
- values: bfloat16 [12288, 2560], P('seq', 'head'), may hold values from -6 to 6
- out_grad: bfloat16 [12288, 2560], P('seq', 'head'), may hold values from -6 to 6
- out_weight: bfloat16 [2560, 2560], P('head'), may hold values from -0.125 to 0.125
- offsets: int32 [32], P('head'), may hold values from 0 to 7, as said below
Outputs:
- query_grad: bfloat16 [12288, 2560], P('seq', 'head')
- key_grad: bfloat16 [12288, 2560], P('seq', 'head')
- value_grad: bfloat16 [12288, 2560], P('seq', 'head')
Inputs may be any that keep to these rules, and one draw needn't show every extreme that they name: offsets[h] is below 2 ** (h mod 4).
All inputs are finite; a program needn't handle non-finite values.
Results may differ from a plain program's by a relative error of at most 0.011.
Values may be sent and summed in bfloat16 or wider, within the bound.
No kernel may reach another device: no remote copies, remote signals or barrier semaphores. Data moves between devices by JAX's collectives and lax.ppermute only.
A program may use at most 128 MiB of HBM per device.

v0:
```python
import functools

import jax
import jax.numpy as jnp
from jax import lax
from jax.experimental import pallas as pl
from jax.experimental.pallas import tpu as pltpu
from jax.sharding import PartitionSpec as P

HEAD_DIM = 80
GROUPS = 4
SLOT = 128
PAIR = 2 * SLOT
NEG = -1e30
PLACE = 4
SCALE = HEAD_DIM ** (-0.5)
LOG2E = 1.4426950408889634
ORDER = {1: (0, 1), 2: (0, 1, 2, 3), 3: (0, 1, 2, 3, 4, 6, 5, 7)}
NT = (((1,), (1,)), ((), ()))
NN = (((1,), (0,)), ((), ()))
TN = (((0,), (0,)), ((), ()))
F32 = jnp.float32
BF16 = jnp.bfloat16


def dot(a, b, dims):
    return lax.dot_general(a, b, dims, preferred_element_type=F32)


def iota(shape, axis):
    return lax.broadcasted_iota(jnp.int32, shape, axis)


def window(head):
    low = HEAD_DIM * head
    start = low // SLOT * SLOT
    width = SLOT if low - start + HEAD_DIM <= SLOT else 2 * SLOT
    return start, width, low - start


def to_slot(x, shift, ones=0):
    if shift:
        x = pltpu.roll(x, x.shape[1] - shift, 1)
    x = x[:, :SLOT]
    lane = iota(x.shape, 1)
    fill = jnp.where(lane < HEAD_DIM + ones, 1.0, 0.0) if ones else 0.0
    return jnp.where(lane < HEAD_DIM, x, fill)


def pick(offset, rows, rate, tok):
    return (iota((rows, tok), 1) == iota((rows, tok), 0) * rate + offset).astype(BF16)


def starts_of(tok):
    rows = [tok >> g for g in range(GROUPS)]
    first = {g: sum(rows[1:g]) for g in range(1, GROUPS)}
    return rows, first


def select_kernel(
    info,
    offs_hbm,
    q_hbm,
    k_hbm,
    v_hbm,
    og_hbm,
    w_hbm,
    s0_ref,
    sall_ref,
    s23_ref,
    pick_scr,
    spread_ref,
    own_ref,
    wt_ref,
    x_scr,
    offs,
    sems,
):
    tok = x_scr.shape[1]
    width = x_scr.shape[2]
    rows, first = starts_of(tok)
    copies = [
        pltpu.make_async_copy(ref, x_scr.at[i], sems.at[i])
        for i, ref in enumerate((q_hbm, k_hbm, v_hbm))
    ]
    scalars = pltpu.make_async_copy(offs_hbm, offs, sems.at[3])
    copies.append(pltpu.make_async_copy(og_hbm, own_ref, sems.at[4]))
    for i in range(4):
        column = pl.ds(pl.multiple_of(info[i] * width, SLOT), width)
        copies.append(pltpu.make_async_copy(w_hbm.at[:, column], wt_ref.at[i], sems.at[5 + i]))
    scalars.start()
    for copy in copies:
        copy.start()
    scalars.wait()
    for a in range(2):
        spread_ref[a] = spread_matrix(offs, a, (1, 2, 3), tok)
        for g in range(1, GROUPS):
            chosen = pick(offs[GROUPS * a + g], rows[g], 1 << g, tok)
            pick_scr[a, first[g] : first[g] + rows[g], :] = chosen
    for i in range(3):
        copies[i].wait()
        for a in range(2):
            col = (2 * i + a) * SLOT
            for g in range(GROUPS):
                start, width, shift = window(GROUPS * a + g)
                x = x_scr[i, :, start : start + width]
                if g == 0:
                    y = to_slot(x.astype(F32), shift, 2 if i == 2 else 0)
                    s0_ref[:, col : col + SLOT] = y.astype(BF16)
                    continue
                at = first[g]
                x = dot(pick_scr[a, at : at + rows[g], :], x, NN)
                y = to_slot(x, shift, 2 if i == 2 else 0).astype(BF16)
                sall_ref[at : at + rows[g], col : col + SLOT] = y
                if g > 1:
                    at -= rows[1]
                    s23_ref[at : at + rows[g], col : col + SLOT] = y
    for copy in copies[3:]:
        copy.wait()


def forward_block(q, k, mask):
    st = jnp.where(mask, dot(k, q, NT), NEG)
    top = jnp.max(st, axis=0, keepdims=True)
    e = jnp.exp2((st - top) * (SCALE * LOG2E))
    total = jnp.sum(e, axis=0, keepdims=True)
    return e * (1.0 / total)


def own_forward_kernel(s0_ref, p_ref, o_ref):
    tok = s0_ref.shape[0]
    for b in range(tok // SLOT):
        lo, hi = b * SLOT, (b + 1) * SLOT
        mask = iota((hi, SLOT), 0) <= iota((hi, SLOT), 1) + lo
        for a in range(2):
            at = a * SLOT
            q = s0_ref[lo:hi, at : at + SLOT]
            k = s0_ref[:hi, PAIR + at : PAIR + at + SLOT]
            v = s0_ref[:hi, 2 * PAIR + at : 2 * PAIR + at + SLOT]
            p = forward_block(q, k, mask).astype(BF16)
            p_ref[a, :hi, lo:hi] = p
            if hi < tok:
                p_ref[a, hi:, lo:hi] = jnp.zeros((tok - hi, SLOT), BF16)
            o_ref[lo:hi, at : at + SLOT] = dot(p, v, TN)


def assemble(g, tok, own, near, r2, r4, r6, d, d2):
    rows, first = starts_of(tok)
    n = rows[g]
    at = first[g]
    low = at - rows[1]
    d4 = d2 + r2.shape[0]
    parts = [(own, at), (near, at)]
    if g > 1:
        parts += [(r2, low), (d, d2 + low)]
    if g > 2:
        parts += [(r4, 0), (r6, 0), (d, d4), (d, d4 + n)]
    return n, parts


def places(g, n, place, shape, axis):
    s = iota(shape, axis)
    code = jnp.zeros(shape, jnp.int32)
    back = jnp.zeros(shape, jnp.int32)
    for i, m in enumerate(ORDER[g]):
        if i:
            code = jnp.where(s >= i * n, m, code)
            back = jnp.where(s >= i * n, i * n, back)
    return (code ^ place) * n + s - back


def segment_forward_kernel(
    info, own, r2, r4, r6, d, f_ref, o1_ref, o23_ref, q1, q2, q3, k1, k2, k3
):
    tok = f_ref.shape[1]
    rows, first = starts_of(tok)
    for g, pq, pk in ((1, q1, k1), (2, q2, k2), (3, q3, k3)):
        n, parts = assemble(g, tok, own, d, r2, r4, r6, d, own.shape[0])
        for i, (ref, at) in enumerate(parts):
            f_ref[g - 1, i * n : (i + 1) * n, :] = ref[at : at + n, :]
        place = lax.rem(info[PLACE], 1 << g)
        at_key = places(g, n, place, (tok, SLOT), 0)
        at_query = places(g, n, place, (1, tok), 1)
        for b in range(tok // SLOT):
            lo, hi = b * SLOT, (b + 1) * SLOT
            mask = at_key <= at_query[:, lo:hi]
            for a in range(2):
                c = a * SLOT
                q = f_ref[g - 1, lo:hi, c : c + SLOT]
                k = f_ref[g - 1, :, PAIR + c : PAIR + c + SLOT]
                p = forward_block(q, k, mask)
                pk[a, :, lo:hi] = p[:n].astype(BF16)
                own_rows = min(n, hi) - lo
                if own_rows > 0:
                    mine = jnp.transpose(p)[:own_rows].astype(BF16)
                    pq[a, lo : lo + own_rows, :] = mine
                    v = f_ref[g - 1, :, 2 * PAIR + c : 2 * PAIR + c + SLOT]
                    o = dot(mine, v, NN)
                    if g == 1:
                        o1_ref[lo : lo + own_rows, c : c + SLOT] = o
                    else:
                        at = first[g] - rows[1] + lo
                        o23_ref[at : at + own_rows, c : c + SLOT] = o


def project_own_kernel(own, wt, acc):
    for b in range(4):
        lo = 2 * HEAD_DIM * b
        acc[b] = dot(own[...], wt[0, lo : lo + 2 * HEAD_DIM], NT)


def project_near_kernel(acc_in, left, right, wt, acc):
    for b in range(4):
        lo = 2 * HEAD_DIM * b
        acc[b] = (
            acc_in[b]
            + dot(left[...], wt[1, lo : lo + 2 * HEAD_DIM], NT)
            + dot(right[...], wt[2, lo : lo + 2 * HEAD_DIM], NT)
        )


def with_delta(g, o):
    delta = jnp.sum(g.astype(BF16).astype(F32) * o, axis=1, keepdims=True)
    high = delta.astype(BF16).astype(F32)
    lane = iota(g.shape, 1)
    g = jnp.where(lane == HEAD_DIM, -high, g)
    return jnp.where(lane == HEAD_DIM + 1, high - delta, g).astype(BF16)


def finish_pairs(b0, acc, far1, far2, wt, x_scr, g_scr):
    half = far1.shape[0]
    x_scr[:half] = far1[...]
    x_scr[half:] = far2[...]
    wide = 2 * HEAD_DIM
    parts = []
    for a in range(2):
        b = 2 * a + b0
        lo = wide * b
        parts.append(acc[b] + dot(x_scr[...], wt[3, lo : lo + wide], NT))
        g_scr[a, :, wide:] = jnp.zeros((2 * half, PAIR - wide), BF16)
    for a in range(2):
        g_scr[a, :, :wide] = parts[a].astype(BF16)


def finish_low_kernel(picks, acc, far1, far2, wt, o23, g23_ref, x_scr, g_scr):
    tok = x_scr.shape[0]
    rows, first = starts_of(tok)
    finish_pairs(1, acc, far1, far2, wt, x_scr, g_scr)
    for g in (2, 3):
        for a in range(2):
            c = a * SLOT
            at = first[g] - rows[1]
            n = rows[g]
            x = dot(picks[a, first[g] : first[g] + n, :], g_scr[a], NN)
            x = to_slot(x, HEAD_DIM * (g - 2))
            g23_ref[at : at + n, c : c + SLOT] = with_delta(x, o23[at : at + n, c : c + SLOT])


def finish_high_kernel(picks, acc, far1, far2, wt, o0, o1, g23, g0_ref, gall_ref, x_scr, g_scr):
    tok = x_scr.shape[0]
    n = tok // 2
    finish_pairs(0, acc, far1, far2, wt, x_scr, g_scr)
    gall_ref[n:, :] = g23[...]
    for a in range(2):
        c = a * SLOT
        x = to_slot(g_scr[a, :, :SLOT].astype(F32), 0)
        g0_ref[:, c : c + SLOT] = with_delta(x, o0[:, c : c + SLOT])
        x = to_slot(dot(picks[a, :n, :], g_scr[a], NN), HEAD_DIM)
        gall_ref[:n, c : c + SLOT] = with_delta(x, o1[:, c : c + SLOT])


def own_backward_kernel(s0_ref, p_ref, g_ref, d_ref, ds_scr):
    tok = s0_ref.shape[0]
    for b in range(tok // SLOT):
        lo, hi = b * SLOT, (b + 1) * SLOT
        for a in range(2):
            at = a * SLOT
            v = s0_ref[:hi, 2 * PAIR + at : 2 * PAIR + at + SLOT]
            x = dot(v, g_ref[lo:hi, at : at + SLOT], NT)
            ds_scr[a, :hi, lo:hi] = (p_ref[a, :hi, lo:hi].astype(F32) * x).astype(BF16)
            if hi < tok:
                ds_scr[a, hi:, lo:hi] = jnp.zeros((tok - hi, SLOT), BF16)
    for a in range(2):
        at = a * SLOT
        q = s0_ref[:, at : at + SLOT]
        k = s0_ref[:, PAIR + at : PAIR + at + SLOT]
        ds = ds_scr[a]
        dq = dot(ds, k, TN) * SCALE
        dk = dot(ds, q, NN) * SCALE
        dv = clear(dot(p_ref[a], g_ref[:, at : at + SLOT], NN))
        d_ref[:, at : at + SLOT] = dq.astype(BF16)
        d_ref[:, PAIR + at : PAIR + at + SLOT] = dk.astype(BF16)
        d_ref[:, 2 * PAIR + at : 2 * PAIR + at + SLOT] = dv.astype(BF16)


def clear(x):
    return jnp.where(iota(x.shape, 1) < HEAD_DIM, x, 0.0)


def shifted_lanes(x, by):
    slot, by = by // SLOT, by % SLOT
    if by == 0:
        return slot, x
    if by + HEAD_DIM <= SLOT:
        return slot, pltpu.roll(x, by, 1)
    return slot, pltpu.roll(jnp.concatenate([x, jnp.zeros_like(x)], 1), by, 1)


def spread_matrix(offs, a, groups, tok):
    rows, _ = starts_of(tok)
    width = sum(rows[g] for g in groups)
    col = iota((1, width), 1)
    at = 0
    target = jnp.zeros((1, width), jnp.int32)
    for g in groups:
        here = (col - at) * (1 << g) + offs[GROUPS * a + g]
        target = jnp.where(col >= at, here, target) if at else here
        at += rows[g]
    return (iota((tok, width), 0) == target).astype(BF16)


def place_rows(b_scr, at, g, a, x):
    n = x.shape[0]
    slot, y = shifted_lanes(x, HEAD_DIM * g + a * (GROUPS * HEAD_DIM % SLOT))
    wide = y.shape[1] // SLOT
    zero = jnp.zeros((n, SLOT), BF16)
    for s in range(3):
        if slot <= s < slot + wide:
            part = y[:, (s - slot) * SLOT : (s - slot + 1) * SLOT].astype(BF16)
        else:
            part = zero
        b_scr[at : at + n, s * SLOT : (s + 1) * SLOT] = part


def store_halves(out_ref, halves, base=None):
    lo, hi = halves
    width = out_ref.shape[1]
    tiles = [lo[:, :SLOT], lo[:, SLOT:PAIR], lo[:, PAIR:] + hi[:, :SLOT]]
    tiles += [hi[:, SLOT:PAIR], hi[:, PAIR:]]
    for i, tile in enumerate(tiles):
        if base is not None:
            tile = tile + base[:, i * SLOT : (i + 1) * SLOT].astype(F32)
        out_ref[:, i * SLOT : (i + 1) * SLOT] = tile.astype(BF16)


def add_own(full, a, x):
    slot, y = shifted_lanes(x.astype(F32), a * (GROUPS * HEAD_DIM % SLOT))
    wide = y.shape[1]
    return jnp.concatenate([full[:, :wide] + y, full[:, wide:]], 1)


def query_kernel(spreads, d_ref, f_ref, gall_ref, q1, q2, q3, out_ref, b_scr):
    tok = out_ref.shape[0]
    rows, first = starts_of(tok)
    chain = [(g, a) for g in (1, 2, 3) for a in range(2)]
    pqs = {1: q1, 2: q2, 3: q3}
    grads = {}
    for g, a in chain:
        c = a * SLOT
        v = f_ref[g - 1, :, 2 * PAIR + c : 2 * PAIR + c + SLOT]
        x = dot(gall_ref[first[g] : first[g] + rows[g], c : c + SLOT], v, NT)
        grads[g, a] = (pqs[g][a].astype(F32) * x).astype(BF16)
    for g, a in chain:
        k = f_ref[g - 1, :, PAIR + a * SLOT : PAIR + (a + 1) * SLOT]
        place_rows(b_scr.at[a], first[g], g, a, dot(grads[g, a], k, NN) * SCALE)
    halves = []
    for a in range(2):
        full = dot(spreads[a], b_scr[a], NN)
        halves.append(add_own(full, a, d_ref[:, a * SLOT : (a + 1) * SLOT]))
    store_halves(out_ref, halves)


def key_value_high_kernel(spreads, d_ref, f_ref, own, near, pk, key_ref, value_ref, g_scr, b_scr):
    tok = key_ref.shape[0]
    n = tok // 2
    g_scr[:n] = own[:n]
    g_scr[n:] = near[:n]
    key_value_rows((1,), tok, f_ref, (g_scr,), {1: pk}, b_scr)
    for i, out_ref in enumerate((key_ref, value_ref)):
        parts = []
        for a in range(2):
            c = (i + 1) * PAIR + a * SLOT
            x = dot(spreads[a, :, :n], b_scr[i, a], NN)
            parts.append(add_own(x, a, d_ref[:, c : c + SLOT]))
        store_halves(out_ref, parts)


def key_value_rows(groups, tok, f_ref, g_scr, pks, b_scr):
    rows, first = starts_of(tok)
    chain = [(g, a) for g in groups for a in range(2)]
    grads = {}
    for g, a in chain:
        c = a * SLOT
        v = f_ref[g - 1, : rows[g], 2 * PAIR + c : 2 * PAIR + c + SLOT]
        x = dot(v, g_scr[g - groups[0]][:, c : c + SLOT], NT)
        grads[g, a] = (pks[g][a].astype(F32) * x).astype(BF16)
    for g, a in chain:
        q = f_ref[g - 1, :, a * SLOT : (a + 1) * SLOT]
        at = first[g] - first[groups[0]]
        place_rows(b_scr.at[0, a], at, g, a, dot(grads[g, a], q, NN) * SCALE)
    for g, a in chain:
        gg = g_scr[g - groups[0]][:, a * SLOT : (a + 1) * SLOT]
        at = first[g] - first[groups[0]]
        place_rows(b_scr.at[1, a], at, g, a, clear(dot(pks[g][a], gg, NN)))


def key_value_low_kernel(
    spreads,
    query_in,
    key_in,
    value_in,
    f_ref,
    own,
    near,
    r2,
    r4,
    r6,
    d,
    k2,
    k3,
    query_out,
    key_out,
    value_out,
    g_scr,
    b_scr,
    key_scr,
    value_scr,
    sems,
):
    tok = key_scr.shape[0]
    n = tok // 2
    copies = [
        pltpu.make_async_copy(x, out, sems.at[i])
        for i, (x, out) in enumerate(
            ((query_in, query_out), (key_scr, key_out), (value_scr, value_out))
        )
    ]
    copies[0].start()
    for g in (2, 3):
        m, parts = assemble(g, tok, own, near, r2, r4, r6, d, 0)
        for i, (ref, at) in enumerate(parts):
            g_scr[g - 2, i * m : (i + 1) * m, :] = ref[at : at + m, :]
    key_value_rows((2, 3), tok, f_ref, (g_scr.at[0], g_scr.at[1]), {2: k2, 3: k3}, b_scr)
    for i, (base, out) in enumerate(((key_in, key_scr), (value_in, value_scr))):
        parts = [dot(spreads[a, :, n:], b_scr[i, a], NN) for a in range(2)]
        store_halves(out, parts, base)
        copies[i + 1].start()
    for copy in copies:
        copy.wait()


VM = pl.BlockSpec(memory_space=pltpu.VMEM)
SM = pl.BlockSpec(memory_space=pltpu.SMEM)
HB = pl.BlockSpec(memory_space=pltpu.HBM)


def shape(*dims, dtype=BF16):
    return jax.ShapeDtypeStruct(dims, dtype)


def scratch(*dims, dtype=BF16):
    return pltpu.VMEM(dims, dtype)


def call(kernel, outs, operands, specs="", scratches=(), name=None, out=VM):
    kinds = {"s": SM, "h": HB, "v": VM}
    operands = [
        pltpu.with_memory_space_constraint(x, pltpu.HBM) if kind == "h" else x
        for x, kind in zip(operands, specs + "v" * len(operands))
    ]
    specs = [kinds[x] for x in specs]
    specs += [VM] * (len(operands) - len(specs))
    return pl.pallas_call(
        kernel,
        out_shape=outs,
        in_specs=specs,
        out_specs=jax.tree.map(lambda _: out, outs),
        scratch_shapes=list(scratches),
        compiler_params=pltpu.CompilerParams(vmem_limit_bytes=20 << 20),
        cost_estimate=pl.CostEstimate(
            flops=0, bytes_accessed=0, transcendentals=0
        ),
        name=name,
    )(*operands)


def on_device(queries, keys, values, out_grad, out_weight, offsets):
    tok, width = queries.shape
    rows, first = starts_of(tok)
    half = tok // 2
    index = lax.axis_index("seq")
    column = lax.axis_index("head")
    n_head = lax.axis_size("head")
    n_seq = lax.axis_size("seq")
    right_way = [(i, (i + 1) % n_head) for i in range(n_head)]
    left_way = [(i, (i - 1) % n_head) for i in range(n_head)]
    dma = pltpu.SemaphoreType.DMA

    def swap(x, mask):
        return lax.ppermute(x, "seq", [(i, i ^ mask) for i in range(n_seq)])

    def after(x, *others):
        return lax.optimization_barrier((x,) + others)[0]

    wide = 2 * HEAD_DIM
    n_all = sum(rows[1:])
    n_low = n_all - rows[1]

    left = lax.ppermute(out_grad, "head", right_way)
    right = lax.ppermute(out_grad, "head", left_way)

    blocks = [column, (column + n_head - 1) % n_head, (column + 1) % n_head]
    blocks += [(column + 2) % n_head, index]
    info = jnp.stack(blocks).astype(jnp.int32)

    s0, sall, s23, picks, spreads, own, wt = call(
        select_kernel,
        (
            shape(tok, 3 * PAIR),
            shape(n_all, 3 * PAIR),
            shape(n_low, 3 * PAIR),
            shape(2, n_all, tok),
            shape(2, tok, n_all),
            shape(tok, width),
            shape(4, width, width),
        ),
        (info, offsets, queries, keys, values, out_grad, out_weight),
        specs="shhhhhh",
        scratches=(scratch(3, tok, width), pltpu.SMEM((2 * GROUPS,), jnp.int32), dma((9,))),
        name="select",
    )

    def far_swaps(low):
        last = low[rows[2] :]
        r4 = swap(last, 4)
        r2 = swap(low, 2)
        return r2, r4, swap(last, 6)

    r2, r4, r6 = far_swaps(s23)
    acc_own = call(
        project_own_kernel,
        shape(4, tok, wide, dtype=F32),
        (own, wt),
        name="project_own",
    )
    p0, o0 = call(
        own_forward_kernel,
        (shape(2, tok, tok), shape(tok, PAIR, dtype=F32)),
        (s0,),
        name="own_forward",
    )
    left, right, acc_own, o0 = lax.optimization_barrier((left, right, acc_own, o0))
    far1 = lax.ppermute(left[:half], "head", right_way)
    far2 = lax.ppermute(right[half:], "head", left_way)
    r2, r4, r6, o0 = lax.optimization_barrier((r2, r4, r6, o0))
    d = swap(jnp.concatenate([sall, r2, r4, r6], 0), 1)
    acc = call(
        project_near_kernel,
        shape(4, tok, wide, dtype=F32),
        (after(acc_own, r2), left, right, wt),
        name="project_near",
    )
    d = after(d, acc)
    seg = call(
        segment_forward_kernel,
        (shape(3, tok, 3 * PAIR), shape(rows[1], PAIR, dtype=F32), shape(n_low, PAIR, dtype=F32))
        + tuple(shape(2, rows[g], tok) for g in (1, 2, 3)) * 2,
        (info, sall, r2, r4, r6, d),
        specs="s",
        name="segment_forward",
    )
    full, o1, o23 = seg[:3]
    pq, pk = seg[3:6], seg[6:9]

    pair_scratch = (scratch(tok, width), scratch(2, tok, PAIR))
    g23 = call(
        finish_low_kernel,
        shape(n_low, PAIR),
        (picks, acc, far1, far2, wt, o23),
        scratches=pair_scratch,
        name="finish_low",
    )
    g_far = far_swaps(g23)
    g0, gall = call(
        finish_high_kernel,
        (shape(tok, PAIR), shape(n_all, PAIR)),
        (picks, acc, far1, far2, wt, o0, o1, g23),
        scratches=pair_scratch,
        name="finish_high",
    )
    g_near = swap(gall, 1)
    d0 = call(
        own_backward_kernel,
        shape(tok, 3 * PAIR),
        (s0, p0, g0),
        scratches=(scratch(2, tok, tok),),
        name="own_backward",
    )
    key_part, value_part = call(
        key_value_high_kernel,
        (shape(tok, width), shape(tok, width)),
        (spreads, d0, full, gall, g_near, pk[0]),
        scratches=(scratch(tok, PAIR), scratch(2, 2, rows[1], 3 * SLOT)),
        name="key_value_high",
    )
    g_far = lax.optimization_barrier(g_far + (key_part,))[:3]
    g_d = swap(jnp.concatenate(g_far, 0), 1)
    query_part = call(
        query_kernel,
        shape(tok, width),
        (spreads, after(d0, g_far[1]), full, gall) + tuple(pq),
        scratches=(scratch(2, n_all, 3 * SLOT),),
        name="query_side",
    )
    return tuple(
        call(
            key_value_low_kernel,
            (shape(tok, width),) * 3,
            (spreads, query_part, key_part, value_part, full, gall, g_near)
            + g_far
            + (g_d,)
            + tuple(pk[1:]),
            scratches=(
                scratch(2, tok, PAIR),
                scratch(2, 2, n_low, 3 * SLOT),
                scratch(tok, width),
                scratch(tok, width),
                dma((3,)),
            ),
            name="key_value_low",
            out=HB,
        )
    )


def solution(mesh):
    placed = (
        P("seq", "head"),
        P("seq", "head"),
        P("seq", "head"),
        P("seq", "head"),
        P("head", None),
        P("head"),
    )
    return jax.shard_map(
        on_device,
        mesh=mesh,
        in_specs=placed,
        out_specs=(P("seq", "head"), P("seq", "head"), P("seq", "head")),
        check_vma=False,
    )
```

profile of v0, /device:TPU:1, one launch (start us, length us, event | category | flops | bytes accessed | tf_op | source)
XLA Modules:
  0.0 43.8 jit_solution(11993961098645269612)
XLA Ops:
  0.6 3.4 %collective-permute-start.1 = (bf16[384,640]{1,0:T(8,128)(2,1)}, bf16[384,640]{1,0:T(8,128)(2,1)S(1)}, u32[]{:S(2)}, u32[]{:S(2)}) collective-permute-start(bf16[384,640]{1,0:T(8,128)(2,1)} %og_hbm.1), channel_id=1, source_target_pairs={{0,3},{1,0},{2,1},{3,2},{4,7},{5,4},{6,5},{7,6},{8,11},{9,8},{10,9... | collective-permute-start | bytes 1474568 | tf_op jit(solution)/shard_map/ppermute | solution.py:510
  4.1 3.1 %select.7 = (bf16[384,768]{1,0:T(8,128)(2,1)S(1)}, bf16[336,768]{1,0:T(8,128)(2,1)S(1)}, bf16[144,768]{1,0:T(8,128)(2,1)S(1)}, bf16[2,336,384]{2,1,0:T(8,128)(2,...) custom-call(s32[5]{0:T(128)S(1)} %stack.23.info, ...), custom_call_target="tpu_custom_call" | custom-call | tf_op jit(solution)/shard_map/select/pallas_call | solution.py:473
  7.2 1.7 %collective-permute-start.2 = (bf16[144,768]{1,0:T(8,128)(2,1)S(1)}, bf16[144,768]{1,0:T(8,128)(2,1)S(1)}, u32[]{:S(2)}, u32[]{:S(2)}) collective-permute-start(bf16[144,768]{1,0:T(8,128)(2,1)S(1)} %get-tuple-element.47), channel_id=1, source_target_pairs={{0,8},{4,12},{8,0},{12,4},{16,24},{20,28},{24,16},{28,20},{32,40},... | collective-permute-start | bytes 663560 | tf_op jit(solution)/shard_map/ppermute | solution.py:500
  8.9 2.2 %collective-permute-start.4 = (bf16[48,768]{1,0:T(8,128)(2,1)S(1)}, bf16[48,768]{1,0:T(8,128)(2,1)S(1)}, u32[]{:S(2)}, u32[]{:S(2)}) collective-permute-start(bf16[48,768]{1,0:T(8,128)(2,1)S(1)} %slice.12), channel_id=1, source_target_pairs={{0,24},{4,28},{8,16},{12,20},{16,8},{20,12},{24,0},{28,4},{32,56},... | collective-permute-start | bytes 221192 | tf_op jit(solution)/shard_map/ppermute | solution.py:500
  11.2 1.1 %collective-permute-start.3 = (bf16[48,768]{1,0:T(8,128)(2,1)S(1)}, bf16[48,768]{1,0:T(8,128)(2,1)S(1)}, u32[]{:S(2)}, u32[]{:S(2)}) collective-permute-start(bf16[48,768]{1,0:T(8,128)(2,1)S(1)} %slice.12), channel_id=1, source_target_pairs={{0,16},{4,20},{8,24},{12,28},{16,0},{20,4},{24,8},{28,12},{32,48},... | collective-permute-start | bytes 221192 | tf_op jit(solution)/shard_map/ppermute | solution.py:500
  12.3 1.4 %own_forward.1 = (bf16[2,384,384]{2,1,0:T(8,128)(2,1)S(1)}, f32[384,256]{1,0:T(8,128)S(1)}) custom-call(bf16[384,768]{1,0:T(8,128)(2,1)S(1)} %get-tuple-element.40.s0_ref), custom_call_target="tpu_custom_call" | custom-call | tf_op jit(solution)/shard_map/own_forward/pallas_call | solution.py:473
  14.6 2.6 %collective-permute-done.left = bf16[384,640]{1,0:T(8,128)(2,1)S(1)} collective-permute-done((bf16[384,640]{1,0:T(8,128)(2,1)}, bf16[384,640]{1,0:T(8,128)(2,1)S(1)}, u32[]{:S(2)}, u32[]{:S(2)}) %collective-permute-start) | collective-permute-done | bytes 491552 | tf_op jit(solution)/shard_map/ppermute | solution.py:509
  17.2 0.8 %collective-permute-done.3.r4 = bf16[48,768]{1,0:T(8,128)(2,1)S(1)} collective-permute-done((bf16[48,768]{1,0:T(8,128)(2,1)S(1)}, bf16[48,768]{1,0:T(8,128)(2,1)S(1)}, u32[]{:S(2)}, u32[]{:S(2)}) %collective-permute-start.3) | collective-permute-done | bytes 73760 | tf_op jit(solution)/shard_map/ppermute | solution.py:500
  18.1 2.2 %collective-permute-start.7 = (bf16[576,768]{1,0:T(8,128)(2,1)S(1)}, bf16[576,768]{1,0:T(8,128)(2,1)S(1)}, u32[]{:S(2)}, u32[]{:S(2)}) collective-permute-start(bf16[576,768]{1,0:T(8,128)(2,1)S(1)} %pad_maximum_fusion), channel_id=1, source_target_pairs={{0,4},{4,0},{8,12},{12,8},{16,20},{20,16},{24,28},{28,24},{32,36},... | collective-permute-start | bytes 2654216 | tf_op jit(solution)/shard_map/ppermute | solution.py:500
  20.7 2.6 %collective-permute-start.6 = (bf16[192,640]{1,0:T(8,128)(2,1)S(1)}, bf16[192,640]{1,0:T(8,128)(2,1)S(1)}, u32[]{:S(2)}, u32[]{:S(2)}) collective-permute-start(bf16[192,640]{1,0:T(8,128)(2,1)S(1)} %slice.14), channel_id=1, source_target_pairs={{0,3},{1,0},{2,1},{3,2},{4,7},{5,4},{6,5},{7,6},{8,11},{9,8},{10,9... | collective-permute-start | bytes 737288 | tf_op jit(solution)/shard_map/ppermute | solution.py:554
  23.2 1.4 %project_near.1.acc = f32[4,384,160]{2,1,0:T(8,128)S(1)} custom-call(f32[4,384,160]{2,1,0:T(8,128)S(1)} %project_own.1.acc_in, bf16[384,640]{1,0:T(8,128)(2,1)S(1)} %collective-permute-done.left, bf16[384,640]{1,0:T(8,128)(2,1)S(1)} %collective-permute-done.1.right, bf16[4,640,640]{2,1,0:T(8,128)(2,1)S(1)} %get-tuple-element.44.wt), custom_call_target="tpu_custom_call" | custom-call | tf_op jit(solution)/shard_map/project_near/pallas_call | solution.py:473
  24.6 2.5 %segment_forward.1 = (bf16[3,384,768]{2,1,0:T(8,128)(2,1)S(1)}, f32[192,256]{1,0:T(8,128)S(1)}, f32[144,256]{1,0:T(8,128)S(1)}, bf16[2,192,384]{2,1,0:T(8,128)(2...) custom-call(s32[5]{0:T(128)S(1)} %stack.23.info, ...), custom_call_target="tpu_custom_call" | custom-call | tf_op jit(solution)/shard_map/segment_forward/pallas_call | solution.py:473
  27.2 2.1 %collective-permute-done.5.far1 = bf16[192,640]{1,0:T(8,128)(2,1)S(1)} collective-permute-done((bf16[192,640]{1,0:T(8,128)(2,1)S(1)}, bf16[192,640]{1,0:T(8,128)(2,1)S(1)}, u32[]{:S(2)}, u32[]{:S(2)}) %collective-permute-start.5) | collective-permute-done | bytes 245792 | tf_op jit(solution)/shard_map/ppermute | solution.py:553
  29.3 0.9 %finish_low.1.g23 = bf16[144,256]{1,0:T(8,128)(2,1)S(1)} custom-call(bf16[2,336,384]{2,1,0:T(8,128)(2,1)S(1)} %get-tuple-element.42.picks, f32[4,384,160]{2,1,0:T(8,128)S(1)} %project_near.1.acc, bf16[192,640]{1,0:T(8,128)(2,1)S(1)} %collective-permute-done.5.far1, bf16[192,640]{1,0:T(8,128)(2,1)S(1)} %collective-permute-done.6.far2, ...), custom_call_target="tpu_custom_call" | custom-call | tf_op jit(solution)/shard_map/finish_low/pallas_call | solution.py:473
  30.2 0.9 %finish_high.1 = (bf16[384,256]{1,0:T(8,128)(2,1)S(1)}, bf16[336,256]{1,0:T(8,128)(2,1)S(1)}) custom-call(bf16[2,336,384]{2,1,0:T(8,128)(2,1)S(1)} %get-tuple-element.42.picks, f32[4,384,160]{2,1,0:T(8,128)S(1)} %project_near.1.acc, bf16[192,640]{1,0:T(8,128)(2,1)S(1)} %collective-permute-done.5.far1, bf16[192,640]{1,0:T(8,128)(2,1)S(1)} %collective-permute-done.6.far2, ...), custom_call_target="tpu_custom_call" | custom-call | tf_op jit(solution)/shard_map/finish_high/pallas_call | solution.py:473
  31.1 0.9 %collective-permute-start.11 = (bf16[336,256]{1,0:T(8,128)(2,1)S(1)}, bf16[336,256]{1,0:T(8,128)(2,1)S(1)}, u32[]{:S(2)}, u32[]{:S(2)}) collective-permute-start(bf16[336,256]{1,0:T(8,128)(2,1)S(1)} %get-tuple-element.62.own.gall_ref), channel_id=1, source_target_pairs={{0,4},{4,0},{8,12},{12,8},{16,20},{20,16},{24,28},{28,24},{32,36},... | collective-permute-start | bytes 516104 | tf_op jit(solution)/shard_map/ppermute | solution.py:500
  32.5 2.2 %collective-permute-start.10 = (bf16[48,256]{1,0:T(8,128)(2,1)S(1)}, bf16[48,256]{1,0:T(8,128)(2,1)S(1)}, u32[]{:S(2)}, u32[]{:S(2)}) collective-permute-start(bf16[48,256]{1,0:T(8,128)(2,1)S(1)} %slice.16), channel_id=1, source_target_pairs={{0,24},{4,28},{8,16},{12,20},{16,8},{20,12},{24,0},{28,4},{32,56},... | collective-permute-start | bytes 73736 | tf_op jit(solution)/shard_map/ppermute | solution.py:500
  34.8 1.1 %collective-permute-start.9 = (bf16[48,256]{1,0:T(8,128)(2,1)S(1)}, bf16[48,256]{1,0:T(8,128)(2,1)S(1)}, u32[]{:S(2)}, u32[]{:S(2)}) collective-permute-start(bf16[48,256]{1,0:T(8,128)(2,1)S(1)} %slice.16), channel_id=1, source_target_pairs={{0,16},{4,20},{8,24},{12,28},{16,0},{20,4},{24,8},{28,12},{32,48},... | collective-permute-start | bytes 73736 | tf_op jit(solution)/shard_map/ppermute | solution.py:500
  35.8 0.9 %own_backward.1.d_ref = bf16[384,768]{1,0:T(8,128)(2,1)S(1)} custom-call(bf16[384,768]{1,0:T(8,128)(2,1)S(1)} %get-tuple-element.40.s0_ref, bf16[2,384,384]{2,1,0:T(8,128)(2,1)S(1)} %get-tuple-element.41.p_ref, bf16[384,256]{1,0:T(8,128)(2,1)S(1)} %get-tuple-element.60.g_ref), custom_call_target="tpu_custom_call" | custom-call | tf_op jit(solution)/shard_map/own_backward/pallas_call | solution.py:473
  36.7 1.0 %key_value_high.1 = (bf16[384,640]{1,0:T(8,128)(2,1)S(1)}, bf16[384,640]{1,0:T(8,128)(2,1)S(1)}) custom-call(bf16[2,384,336]{2,1,0:T(8,128)(2,1)S(1)} %get-tuple-element.39.spreads, bf16[384,768]{1,0:T(8,128)(2,1)S(1)} %own_backward.1.d_ref, bf16[3,384,768]{2,1,0:T(8,128)(2,1)S(1)} %get-tuple-element.61.f_ref, ...), custom_call_target="tpu_custom_call" | custom-call | tf_op jit(solution)/shard_map/key_value_high/pallas_call | solution.py:473
  37.7 1.2 %collective-permute-done.9.r4 = bf16[48,256]{1,0:T(8,128)(2,1)S(1)} collective-permute-done((bf16[48,256]{1,0:T(8,128)(2,1)S(1)}, bf16[48,256]{1,0:T(8,128)(2,1)S(1)}, u32[]{:S(2)}, u32[]{:S(2)}) %collective-permute-start.9) | collective-permute-done | bytes 24608 | tf_op jit(solution)/shard_map/ppermute | solution.py:500
  39.0 1.9 %collective-permute-start.12 = (bf16[240,256]{1,0:T(8,128)(2,1)S(1)}, bf16[240,256]{1,0:T(8,128)(2,1)S(1)}, u32[]{:S(2)}, u32[]{:S(2)}) collective-permute-start(bf16[240,256]{1,0:T(8,128)(2,1)S(1)} %pad_maximum_fusion.1), channel_id=1, source_target_pairs={{0,4},{4,0},{8,12},{12,8},{16,20},{20,16},{24,28},{28,24},{32,36},... | collective-permute-start | bytes 368648 | tf_op jit(solution)/shard_map/ppermute | solution.py:500
  40.8 1.1 %query_side.1.query_in = bf16[384,640]{1,0:T(8,128)(2,1)S(1)} custom-call(bf16[2,384,336]{2,1,0:T(8,128)(2,1)S(1)} %get-tuple-element.39.spreads, bf16[384,768]{1,0:T(8,128)(2,1)S(1)} %own_backward.1.d_ref, bf16[3,384,768]{2,1,0:T(8,128)(2,1)S(1)} %get-tuple-element.61.f_ref, bf16[336,256]{1,0:T(8,128)(2,1)S(1)} %get-tuple-element.62.own.gall_ref, ...), custom_call_target="tpu_custom_call" | custom-call | tf_op jit(solution)/shard_map/query_side/pallas_call | solution.py:473
  42.0 1.9 %key_value_low.1 = (bf16[384,640]{1,0:T(8,128)(2,1)}, bf16[384,640]{1,0:T(8,128)(2,1)}, bf16[384,640]{1,0:T(8,128)(2,1)}) custom-call(bf16[2,384,336]{2,1,0:T(8,128)(2,1)S(1)} %get-tuple-element.39.spreads, bf16[384,640]{1,0:T(8,128)(2,1)S(1)} %query_side.1.query_in, bf16[384,640]{1,0:T(8,128)(2,1)S(1)} %get-tuple-element.64.key_in, ...), custom_call_target="tpu_custom_call" | custom-call | tf_op jit(solution)/shard_map/key_value_low/pallas_call | solution.py:473
  (20 shorter events, 1.8 us)
Async XLA Ops:
  0.6 13.9 %collective-permute-start.1 = (bf16[384,640]{1,0:T(8,128)(2,1)}, bf16[384,640]{1,0:T(8,128)(2,1)S(1)}, u32[]{:S(2)}, u32[]{:S(2)}) collective-permute-start(bf16[384,640]{1,0:T(8,128)(2,1)} %og_hbm.1), channel_id=1, source_target_pairs={{0,3},{1,0},{2,1},{3,2},{4,7},{5,4},{6,5},{7,6},{8,11},{9,8},{10,9... | collective-permute-start | bytes 1474568 | tf_op jit(solution)/shard_map/ppermute | solution.py:510
  4.0 13.2 %collective-permute-start = (bf16[384,640]{1,0:T(8,128)(2,1)}, bf16[384,640]{1,0:T(8,128)(2,1)S(1)}, u32[]{:S(2)}, u32[]{:S(2)}) collective-permute-start(bf16[384,640]{1,0:T(8,128)(2,1)} %og_hbm.1), channel_id=1, source_target_pairs={{0,1},{1,2},{2,3},{3,0},{4,5},{5,6},{6,7},{7,4},{8,9},{9,10},{10,1... | collective-permute-start | bytes 1474568 | tf_op jit(solution)/shard_map/ppermute | solution.py:509
  7.2 10.8 %collective-permute-start.2 = (bf16[144,768]{1,0:T(8,128)(2,1)S(1)}, bf16[144,768]{1,0:T(8,128)(2,1)S(1)}, u32[]{:S(2)}, u32[]{:S(2)}) collective-permute-start(bf16[144,768]{1,0:T(8,128)(2,1)S(1)} %get-tuple-element.47), channel_id=1, source_target_pairs={{0,8},{4,12},{8,0},{12,4},{16,24},{20,28},{24,16},{28,20},{32,40},... | collective-permute-start | bytes 663560 | tf_op jit(solution)/shard_map/ppermute | solution.py:500
  8.9 8.3 %collective-permute-start.4 = (bf16[48,768]{1,0:T(8,128)(2,1)S(1)}, bf16[48,768]{1,0:T(8,128)(2,1)S(1)}, u32[]{:S(2)}, u32[]{:S(2)}) collective-permute-start(bf16[48,768]{1,0:T(8,128)(2,1)S(1)} %slice.12), channel_id=1, source_target_pairs={{0,24},{4,28},{8,16},{12,20},{16,8},{20,12},{24,0},{28,4},{32,56},... | collective-permute-start | bytes 221192 | tf_op jit(solution)/shard_map/ppermute | solution.py:500
  11.2 6.8 %collective-permute-start.3 = (bf16[48,768]{1,0:T(8,128)(2,1)S(1)}, bf16[48,768]{1,0:T(8,128)(2,1)S(1)}, u32[]{:S(2)}, u32[]{:S(2)}) collective-permute-start(bf16[48,768]{1,0:T(8,128)(2,1)S(1)} %slice.12), channel_id=1, source_target_pairs={{0,16},{4,20},{8,24},{12,28},{16,0},{20,4},{24,8},{28,12},{32,48},... | collective-permute-start | bytes 221192 | tf_op jit(solution)/shard_map/ppermute | solution.py:500
  18.1 6.5 %collective-permute-start.7 = (bf16[576,768]{1,0:T(8,128)(2,1)S(1)}, bf16[576,768]{1,0:T(8,128)(2,1)S(1)}, u32[]{:S(2)}, u32[]{:S(2)}) collective-permute-start(bf16[576,768]{1,0:T(8,128)(2,1)S(1)} %pad_maximum_fusion), channel_id=1, source_target_pairs={{0,4},{4,0},{8,12},{12,8},{16,20},{20,16},{24,28},{28,24},{32,36},... | collective-permute-start | bytes 2654216 | tf_op jit(solution)/shard_map/ppermute | solution.py:500
  20.4 8.9 %collective-permute-start.5 = (bf16[192,640]{1,0:T(8,128)(2,1)S(1)}, bf16[192,640]{1,0:T(8,128)(2,1)S(1)}, u32[]{:S(2)}, u32[]{:S(2)}) collective-permute-start(bf16[192,640]{1,0:T(8,128)(2,1)S(1)} %slice.13), channel_id=1, source_target_pairs={{0,1},{1,2},{2,3},{3,0},{4,5},{5,6},{6,7},{7,4},{8,9},{9,10},{10,1... | collective-permute-start | bytes 737288 | tf_op jit(solution)/shard_map/ppermute | solution.py:553
  20.7 8.6 %collective-permute-start.6 = (bf16[192,640]{1,0:T(8,128)(2,1)S(1)}, bf16[192,640]{1,0:T(8,128)(2,1)S(1)}, u32[]{:S(2)}, u32[]{:S(2)}) collective-permute-start(bf16[192,640]{1,0:T(8,128)(2,1)S(1)} %slice.14), channel_id=1, source_target_pairs={{0,3},{1,0},{2,1},{3,2},{4,7},{5,4},{6,5},{7,6},{8,11},{9,8},{10,9... | collective-permute-start | bytes 737288 | tf_op jit(solution)/shard_map/ppermute | solution.py:554
  31.1 5.6 %collective-permute-start.11 = (bf16[336,256]{1,0:T(8,128)(2,1)S(1)}, bf16[336,256]{1,0:T(8,128)(2,1)S(1)}, u32[]{:S(2)}, u32[]{:S(2)}) collective-permute-start(bf16[336,256]{1,0:T(8,128)(2,1)S(1)} %get-tuple-element.62.own.gall_ref), channel_id=1, source_target_pairs={{0,4},{4,0},{8,12},{12,8},{16,20},{20,16},{24,28},{28,24},{32,36},... | collective-permute-start | bytes 516104 | tf_op jit(solution)/shard_map/ppermute | solution.py:500
  32.0 7.0 %collective-permute-start.8 = (bf16[144,256]{1,0:T(8,128)(2,1)S(1)}, bf16[144,256]{1,0:T(8,128)(2,1)S(1)}, u32[]{:S(2)}, u32[]{:S(2)}) collective-permute-start(bf16[144,256]{1,0:T(8,128)(2,1)S(1)} %finish_low.1.g23), channel_id=1, source_target_pairs={{0,8},{4,12},{8,0},{12,4},{16,24},{20,28},{24,16},{28,20},{32,40},... | collective-permute-start | bytes 221192 | tf_op jit(solution)/shard_map/ppermute | solution.py:500
  32.5 5.2 %collective-permute-start.10 = (bf16[48,256]{1,0:T(8,128)(2,1)S(1)}, bf16[48,256]{1,0:T(8,128)(2,1)S(1)}, u32[]{:S(2)}, u32[]{:S(2)}) collective-permute-start(bf16[48,256]{1,0:T(8,128)(2,1)S(1)} %slice.16), channel_id=1, source_target_pairs={{0,24},{4,28},{8,16},{12,20},{16,8},{20,12},{24,0},{28,4},{32,56},... | collective-permute-start | bytes 73736 | tf_op jit(solution)/shard_map/ppermute | solution.py:500
  34.8 4.2 %collective-permute-start.9 = (bf16[48,256]{1,0:T(8,128)(2,1)S(1)}, bf16[48,256]{1,0:T(8,128)(2,1)S(1)}, u32[]{:S(2)}, u32[]{:S(2)}) collective-permute-start(bf16[48,256]{1,0:T(8,128)(2,1)S(1)} %slice.16), channel_id=1, source_target_pairs={{0,16},{4,20},{8,24},{12,28},{16,0},{20,4},{24,8},{28,12},{32,48},... | collective-permute-start | bytes 73736 | tf_op jit(solution)/shard_map/ppermute | solution.py:500
  39.0 3.0 %collective-permute-start.12 = (bf16[240,256]{1,0:T(8,128)(2,1)S(1)}, bf16[240,256]{1,0:T(8,128)(2,1)S(1)}, u32[]{:S(2)}, u32[]{:S(2)}) collective-permute-start(bf16[240,256]{1,0:T(8,128)(2,1)S(1)} %pad_maximum_fusion.1), channel_id=1, source_target_pairs={{0,4},{4,0},{8,12},{12,8},{16,20},{20,16},{24,28},{28,24},{32,36},... | collective-permute-start | bytes 368648 | tf_op jit(solution)/shard_map/ppermute | solution.py:500
where the time goes:
time: 43.9 us; the launch traced here: 43.8 us
  starting transfers between devices  20.1 us (46%)
  Pallas kernels  15.9 us (36%)
  waiting for transfers between devices  6.78 us (15%)
  between operations  0.77 us (2%)
    pallas_call x11, Pallas kernels, call(): pl.pallas_call(kernel, out_shape=outs, in_specs=specs, out_specs=jax.tree...  15.9 us
    ppermute x9, starting transfers between devices, swap(): return lax.ppermute(x, 'seq', [(i, i ^ mask) for i in range(n_seq)])  13.9 us
    ppermute x1, starting transfers between devices, on_device(): right = lax.ppermute(out_grad, 'head', left_way)  3.38 us
    ppermute x1, waiting for transfers between devices, on_device(): left = lax.ppermute(out_grad, 'head', right_way)  2.63 us
    ppermute x1, starting transfers between devices, on_device(): far2 = lax.ppermute(right[half:], 'head', left_way)  2.56 us
    ppermute x1, waiting for transfers between devices, on_device(): far1 = lax.ppermute(left[:half], 'head', right_way)  2.08 us
    ppermute x9, waiting for transfers between devices, swap(): return lax.ppermute(x, 'seq', [(i, i ^ mask) for i in range(n_seq)])  2.06 us
  transfers between devices with their start and end apart: 13, of which 4 were waited for; matrix products, arithmetic and copies ran while one was open for 0% of the time, Pallas kernels for 28%

commit v1 on v0

--- a/solution.py
+++ b/solution.py
@@ -11,6 +11,7 @@
 GROUPS = 4
 SLOT = 128
 PAIR = 2 * SLOT
+SPARE = SLOT - HEAD_DIM
 NEG = -1e30
 PLACE = 4
 SCALE = HEAD_DIM ** (-0.5)
@@ -100,21 +101,29 @@
     for i in range(3):
         copies[i].wait()
         for a in range(2):
-            col = (2 * i + a) * SLOT
             for g in range(GROUPS):
                 start, width, shift = window(GROUPS * a + g)
                 x = x_scr[i, :, start : start + width]
                 if g == 0:
+                    col = (2 * i + a) * SLOT
                     y = to_slot(x.astype(F32), shift, 2 if i == 2 else 0)
                     s0_ref[:, col : col + SLOT] = y.astype(BF16)
                     continue
-                at = first[g]
-                x = dot(pick_scr[a, at : at + rows[g], :], x, NN)
-                y = to_slot(x, shift, 2 if i == 2 else 0).astype(BF16)
-                sall_ref[at : at + rows[g], col : col + SLOT] = y
-                if g > 1:
-                    at -= rows[1]
-                    s23_ref[at : at + rows[g], col : col + SLOT] = y
+                at, n = first[g], rows[g]
+                y = to_slot(dot(pick_scr[a, at : at + n, :], x, NN), shift)
+                if i < 2:
+                    col = (2 * i + a) * SLOT
+                    sall_ref[at : at + n, col : col + SLOT] = y.astype(BF16)
+                    continue
+                for half, by in ((0, HEAD_DIM), (1, HEAD_DIM - SPARE)):
+                    col = (2 * a + half) * SLOT
+                    spare = pltpu.roll(y, by, 1).astype(BF16)
+                    lane = iota((n, SLOT), 1)
+                    y_old = sall_ref[at : at + n, col : col + SLOT]
+                    sall_ref[at : at + n, col : col + SLOT] = jnp.where(
+                        lane < HEAD_DIM, y_old, spare
+                    )
+    s23_ref[...] = sall_ref[rows[1] :, :]
     for copy in copies[3:]:
         copy.wait()
 
@@ -144,18 +153,29 @@
             o_ref[lo:hi, at : at + SLOT] = dot(p, v, TN)
 
 
-def assemble(g, tok, own, near, r2, r4, r6, d, d2):
+def parts_of(g, tok, own, near, r2, d2, r4, r6, d4, d6):
     rows, first = starts_of(tok)
-    n = rows[g]
-    at = first[g]
-    low = at - rows[1]
-    d4 = d2 + r2.shape[0]
-    parts = [(own, at), (near, at)]
-    if g > 1:
-        parts += [(r2, low), (d, d2 + low)]
-    if g > 2:
-        parts += [(r4, 0), (r6, 0), (d, d4), (d, d4 + n)]
-    return n, parts
+    low = first[g] - rows[1]
+
+    def at(source):
+        return source[0], source[1] + low
+
+    parts = [at(own), at(near), at(r2), at(d2)]
+    return parts + [r4, r6, d4, d6] if g > 2 else parts
+
+
+def unpack(out, at, x):
+    n = x.shape[0]
+    lane = iota((n, SLOT), 1)
+    tiles = [x[:, i * SLOT : (i + 1) * SLOT].astype(F32) for i in range(4)]
+    slots = [jnp.where(lane < HEAD_DIM, t, 0.0) for t in tiles]
+    ones = jnp.where(lane < HEAD_DIM + 2, 1.0, 0.0)
+    for a in range(2):
+        low = pltpu.roll(tiles[2 * a], SPARE, 1)
+        high = pltpu.roll(tiles[2 * a + 1], SLOT - HEAD_DIM + SPARE, 1)
+        slots.append(jnp.where(lane < SPARE, low, jnp.where(lane < HEAD_DIM, high, ones)))
+    for i, slot in enumerate(slots):
+        out[at : at + n, i * SLOT : (i + 1) * SLOT] = slot.astype(BF16)
 
 
 def places(g, n, place, shape, axis):
@@ -170,14 +190,19 @@
 
 
 def segment_forward_kernel(
-    info, own, r2, r4, r6, d, f_ref, o1_ref, o23_ref, q1, q2, q3, k1, k2, k3
+    info, own, near1, da, r2, r4, r6, db, f_ref, o1_ref, o23_ref, q1, q2, q3, k1, k2, k3
 ):
     tok = f_ref.shape[1]
     rows, first = starts_of(tok)
     for g, pq, pk in ((1, q1, k1), (2, q2, k2), (3, q3, k3)):
-        n, parts = assemble(g, tok, own, d, r2, r4, r6, d, own.shape[0])
+        n, low = rows[g], r2.shape[0]
+        parts = [(own, 0), (near1, 0)]
+        if g > 1:
+            parts = parts_of(
+                g, tok, (own, rows[1]), (da, 0), (r2, 0), (db, 0), (r4, 0), (r6, 0), (db, low), (da, low)
+            )
         for i, (ref, at) in enumerate(parts):
-            f_ref[g - 1, i * n : (i + 1) * n, :] = ref[at : at + n, :]
+            unpack(f_ref.at[g - 1], i * n, ref[at : at + n, :])
         place = lax.rem(info[PLACE], 1 << g)
         at_key = places(g, n, place, (tok, SLOT), 0)
         at_query = places(g, n, place, (1, tok), 1)
@@ -256,17 +281,16 @@
             g23_ref[at : at + n, c : c + SLOT] = with_delta(x, o23[at : at + n, c : c + SLOT])
 
 
-def finish_high_kernel(picks, acc, far1, far2, wt, o0, o1, g23, g0_ref, gall_ref, x_scr, g_scr):
+def finish_high_kernel(picks, acc, far1, far2, wt, o0, o1, g0_ref, g1_ref, x_scr, g_scr):
     tok = x_scr.shape[0]
     n = tok // 2
     finish_pairs(0, acc, far1, far2, wt, x_scr, g_scr)
-    gall_ref[n:, :] = g23[...]
     for a in range(2):
         c = a * SLOT
         x = to_slot(g_scr[a, :, :SLOT].astype(F32), 0)
         g0_ref[:, c : c + SLOT] = with_delta(x, o0[:, c : c + SLOT])
         x = to_slot(dot(picks[a, :n, :], g_scr[a], NN), HEAD_DIM)
-        gall_ref[:n, c : c + SLOT] = with_delta(x, o1[:, c : c + SLOT])
+        g1_ref[:, c : c + SLOT] = with_delta(x, o1[:, c : c + SLOT])
 
 
 def own_backward_kernel(s0_ref, p_ref, g_ref, d_ref, ds_scr):
@@ -349,7 +373,7 @@
     return jnp.concatenate([full[:, :wide] + y, full[:, wide:]], 1)
 
 
-def query_kernel(spreads, d_ref, f_ref, gall_ref, q1, q2, q3, out_ref, b_scr):
+def query_kernel(spreads, d_ref, f_ref, g1_ref, g23_ref, q1, q2, q3, out_ref, b_scr):
     tok = out_ref.shape[0]
     rows, first = starts_of(tok)
     chain = [(g, a) for g in (1, 2, 3) for a in range(2)]
@@ -358,7 +382,9 @@
     for g, a in chain:
         c = a * SLOT
         v = f_ref[g - 1, :, 2 * PAIR + c : 2 * PAIR + c + SLOT]
-        x = dot(gall_ref[first[g] : first[g] + rows[g], c : c + SLOT], v, NT)
+        at = first[g] - rows[1]
+        gg = g1_ref[...] if g == 1 else g23_ref[at : at + rows[g], :]
+        x = dot(gg[:, c : c + SLOT], v, NT)
         grads[g, a] = (pqs[g][a].astype(F32) * x).astype(BF16)
     for g, a in chain:
         k = f_ref[g - 1, :, PAIR + a * SLOT : PAIR + (a + 1) * SLOT]
@@ -373,8 +399,8 @@
 def key_value_high_kernel(spreads, d_ref, f_ref, own, near, pk, key_ref, value_ref, g_scr, b_scr):
     tok = key_ref.shape[0]
     n = tok // 2
-    g_scr[:n] = own[:n]
-    g_scr[n:] = near[:n]
+    g_scr[:n] = own[...]
+    g_scr[n:] = near[...]
     key_value_rows((1,), tok, f_ref, (g_scr,), {1: pk}, b_scr)
     for i, out_ref in enumerate((key_ref, value_ref)):
         parts = []
@@ -411,7 +437,6 @@
     value_in,
     f_ref,
     own,
-    near,
     r2,
     r4,
     r6,
@@ -437,7 +462,19 @@
     ]
     copies[0].start()
     for g in (2, 3):
-        m, parts = assemble(g, tok, own, near, r2, r4, r6, d, 0)
+        m, low = tok >> g, r2.shape[0]
+        parts = parts_of(
+            g,
+            tok,
+            (own, 0),
+            (d, 0),
+            (r2, 0),
+            (d, low),
+            (r4, 0),
+            (r6, 0),
+            (d, 2 * low),
+            (d, 2 * low + r4.shape[0]),
+        )
         for i, (ref, at) in enumerate(parts):
             g_scr[g - 2, i * m : (i + 1) * m, :] = ref[at : at + m, :]
     key_value_rows((2, 3), tok, f_ref, (g_scr.at[0], g_scr.at[1]), {2: k2, 3: k3}, b_scr)
@@ -517,8 +554,8 @@
         select_kernel,
         (
             shape(tok, 3 * PAIR),
-            shape(n_all, 3 * PAIR),
-            shape(n_low, 3 * PAIR),
+            shape(n_all, 2 * PAIR),
+            shape(n_low, 2 * PAIR),
             shape(2, n_all, tok),
             shape(2, tok, n_all),
             shape(tok, width),
@@ -553,19 +590,20 @@
     far1 = lax.ppermute(left[:half], "head", right_way)
     far2 = lax.ppermute(right[half:], "head", left_way)
     r2, r4, r6, o0 = lax.optimization_barrier((r2, r4, r6, o0))
-    d = swap(jnp.concatenate([sall, r2, r4, r6], 0), 1)
+    near1 = swap(after(sall, o0)[: rows[1]], 1)
+    da = swap(jnp.concatenate([s23, r6], 0), 1)
+    db = swap(jnp.concatenate([r2, r4], 0), 1)
     acc = call(
         project_near_kernel,
         shape(4, tok, wide, dtype=F32),
         (after(acc_own, r2), left, right, wt),
         name="project_near",
     )
-    d = after(d, acc)
     seg = call(
         segment_forward_kernel,
         (shape(3, tok, 3 * PAIR), shape(rows[1], PAIR, dtype=F32), shape(n_low, PAIR, dtype=F32))
         + tuple(shape(2, rows[g], tok) for g in (1, 2, 3)) * 2,
-        (info, sall, r2, r4, r6, d),
+        (info, sall, near1, da, r2, r4, r6, db),
         specs="s",
         name="segment_forward",
     )
@@ -581,14 +619,14 @@
         name="finish_low",
     )
     g_far = far_swaps(g23)
-    g0, gall = call(
+    g0, g1 = call(
         finish_high_kernel,
-        (shape(tok, PAIR), shape(n_all, PAIR)),
-        (picks, acc, far1, far2, wt, o0, o1, g23),
+        (shape(tok, PAIR), shape(rows[1], PAIR)),
+        (picks, acc, far1, far2, wt, o0, o1),
         scratches=pair_scratch,
         name="finish_high",
     )
-    g_near = swap(gall, 1)
+    g_near = swap(g1, 1)
     d0 = call(
         own_backward_kernel,
         shape(tok, 3 * PAIR),
@@ -596,19 +634,19 @@
         scratches=(scratch(2, tok, tok),),
         name="own_backward",
     )
+    g_far = lax.optimization_barrier(g_far + (d0,))[:3]
+    g_d = swap(jnp.concatenate((g23,) + g_far, 0), 1)
     key_part, value_part = call(
         key_value_high_kernel,
         (shape(tok, width), shape(tok, width)),
-        (spreads, d0, full, gall, g_near, pk[0]),
+        (spreads, after(d0, g_far[1]), full, g1, g_near, pk[0]),
         scratches=(scratch(tok, PAIR), scratch(2, 2, rows[1], 3 * SLOT)),
         name="key_value_high",
     )
-    g_far = lax.optimization_barrier(g_far + (key_part,))[:3]
-    g_d = swap(jnp.concatenate(g_far, 0), 1)
     query_part = call(
         query_kernel,
         shape(tok, width),
-        (spreads, after(d0, g_far[1]), full, gall) + tuple(pq),
+        (spreads, after(d0, g_far[1]), full, g1, g23) + tuple(pq),
         scratches=(scratch(2, n_all, 3 * SLOT),),
         name="query_side",
     )
@@ -616,7 +654,7 @@
         call(
             key_value_low_kernel,
             (shape(tok, width),) * 3,
-            (spreads, query_part, key_part, value_part, full, gall, g_near)
+            (spreads, query_part, key_part, value_part, full, g23)
             + g_far
             + (g_d,)
             + tuple(pk[1:]),

time: 43.9 us -> 43.1 us (0.982)
  waiting for transfers between devices: 6.78 us -> 4.05 us
  starting transfers between devices: 20.1 us -> 21.4 us
  Pallas kernels: 15.9 us -> 16.4 us
    ppermute x1, waiting for transfers between devices: 2.08 us -> 0.01 us  [on_device(): far1 = lax.ppermute(left[:half], 'head', right_way)]
    ppermute x9 -> x11, starting transfers between devices: 13.9 us -> 15.3 us  [swap(): return lax.ppermute(x, 'seq', [(i, i ^ mask) for i in range(n_seq)])]
    ppermute x9 -> x11, waiting for transfers between devices: 2.06 us -> 1.4 us  [swap(): return lax.ppermute(x, 'seq', [(i, i ^ mask) for i in range(n_seq)])]
  transfers between devices with their start and end apart: 13 -> 15, of which waited for: 4 -> 3; matrix products, arithmetic and copies ran while one was open for 0% -> 0% of each run, Pallas kernels for 28% -> 32%
where the time goes in v1:
time: 43.1 us; the launch traced here: 43 us
  starting transfers between devices  21.4 us (50%)
  Pallas kernels  16.4 us (38%)
  waiting for transfers between devices  4.05 us (9%)
  between operations  0.99 us (2%)
    pallas_call x11, Pallas kernels, call(): pl.pallas_call(kernel, out_shape=outs, in_specs=specs, out_specs=jax.tree...  16.4 us
    ppermute x11, starting transfers between devices, swap(): return lax.ppermute(x, 'seq', [(i, i ^ mask) for i in range(n_seq)])  15.3 us
    ppermute x1, starting transfers between devices, on_device(): right = lax.ppermute(out_grad, 'head', left_way)  3.38 us
    ppermute x1, starting transfers between devices, on_device(): far2 = lax.ppermute(right[half:], 'head', left_way)  2.66 us
    ppermute x1, waiting for transfers between devices, on_device(): left = lax.ppermute(out_grad, 'head', right_way)  2.65 us
    ppermute x11, waiting for transfers between devices, swap(): return lax.ppermute(x, 'seq', [(i, i ^ mask) for i in range(n_seq)])  1.4 us
  transfers between devices with their start and end apart: 15, of which 3 were waited for; matrix products, arithmetic and copies ran while one was open for 0% of the time, Pallas kernels for 32%

profile of v1, /device:TPU:1, one launch (start us, length us, event | category | flops | bytes accessed | tf_op | source)
XLA Modules:
  0.0 43.0 jit_solution(5973461063562996456)
XLA Ops:
  0.6 3.4 %collective-permute-start.1 = (bf16[384,640]{1,0:T(8,128)(2,1)}, bf16[384,640]{1,0:T(8,128)(2,1)S(1)}, u32[]{:S(2)}, u32[]{:S(2)}) collective-permute-start(bf16[384,640]{1,0:T(8,128)(2,1)} %og_hbm.1), channel_id=1, source_target_pairs={{0,3},{1,0},{2,1},{3,2},{4,7},{5,4},{6,5},{7,6},{8,11},{9,8},{10,9... | collective-permute-start | bytes 1474568 | tf_op jit(solution)/shard_map/ppermute | solution.py:547
  4.1 3.1 %select.7 = (bf16[384,768]{1,0:T(8,128)(2,1)S(1)}, bf16[336,512]{1,0:T(8,128)(2,1)S(1)}, bf16[144,512]{1,0:T(8,128)(2,1)S(1)}, bf16[2,336,384]{2,1,0:T(8,128)(2,...) custom-call(s32[5]{0:T(128)S(1)} %stack.23.info, ...), custom_call_target="tpu_custom_call" | custom-call | tf_op jit(solution)/shard_map/select/pallas_call | solution.py:510
  7.2 1.7 %collective-permute-start.2 = (bf16[144,512]{1,0:T(8,128)(2,1)S(1)}, bf16[144,512]{1,0:T(8,128)(2,1)S(1)}, u32[]{:S(2)}, u32[]{:S(2)}) collective-permute-start(bf16[144,512]{1,0:T(8,128)(2,1)S(1)} %get-tuple-element.47), channel_id=1, source_target_pairs={{0,8},{4,12},{8,0},{12,4},{16,24},{20,28},{24,16},{28,20},{32,40},... | collective-permute-start | bytes 442376 | tf_op jit(solution)/shard_map/ppermute | solution.py:537
  8.9 2.2 %collective-permute-start.4 = (bf16[48,512]{1,0:T(8,128)(2,1)S(1)}, bf16[48,512]{1,0:T(8,128)(2,1)S(1)}, u32[]{:S(2)}, u32[]{:S(2)}) collective-permute-start(bf16[48,512]{1,0:T(8,128)(2,1)S(1)} %slice.15), channel_id=1, source_target_pairs={{0,24},{4,28},{8,16},{12,20},{16,8},{20,12},{24,0},{28,4},{32,56},... | collective-permute-start | bytes 147464 | tf_op jit(solution)/shard_map/ppermute | solution.py:537
  11.2 1.1 %collective-permute-start.3 = (bf16[48,512]{1,0:T(8,128)(2,1)S(1)}, bf16[48,512]{1,0:T(8,128)(2,1)S(1)}, u32[]{:S(2)}, u32[]{:S(2)}) collective-permute-start(bf16[48,512]{1,0:T(8,128)(2,1)S(1)} %slice.15), channel_id=1, source_target_pairs={{0,16},{4,20},{8,24},{12,28},{16,0},{20,4},{24,8},{28,12},{32,48},... | collective-permute-start | bytes 147464 | tf_op jit(solution)/shard_map/ppermute | solution.py:537
  12.3 1.4 %own_forward.1 = (bf16[2,384,384]{2,1,0:T(8,128)(2,1)S(1)}, f32[384,256]{1,0:T(8,128)S(1)}) custom-call(bf16[384,768]{1,0:T(8,128)(2,1)S(1)} %get-tuple-element.40.s0_ref), custom_call_target="tpu_custom_call" | custom-call | tf_op jit(solution)/shard_map/own_forward/pallas_call | solution.py:510
  13.8 0.8 %project_own.1.acc_in = f32[4,384,160]{2,1,0:T(8,128)S(1)} custom-call(bf16[384,640]{1,0:T(8,128)(2,1)S(1)} %get-tuple-element.43.own, bf16[4,640,640]{2,1,0:T(8,128)(2,1)S(1)} %get-tuple-element.44.wt), custom_call_target="tpu_custom_call" | custom-call | tf_op jit(solution)/shard_map/project_own/pallas_call | solution.py:510
  14.6 2.6 %collective-permute-done.left = bf16[384,640]{1,0:T(8,128)(2,1)S(1)} collective-permute-done((bf16[384,640]{1,0:T(8,128)(2,1)}, bf16[384,640]{1,0:T(8,128)(2,1)S(1)}, u32[]{:S(2)}, u32[]{:S(2)}) %collective-permute-start) | collective-permute-done | bytes 491552 | tf_op jit(solution)/shard_map/ppermute | solution.py:546
  17.4 2.7 %collective-permute-start.6 = (bf16[192,640]{1,0:T(8,128)(2,1)S(1)}, bf16[192,640]{1,0:T(8,128)(2,1)S(1)}, u32[]{:S(2)}, u32[]{:S(2)}) collective-permute-start(bf16[192,640]{1,0:T(8,128)(2,1)S(1)} %slice.17), channel_id=1, source_target_pairs={{0,3},{1,0},{2,1},{3,2},{4,7},{5,4},{6,5},{7,6},{8,11},{9,8},{10,9... | collective-permute-start | bytes 737288 | tf_op jit(solution)/shard_map/ppermute | solution.py:591
  20.1 2.5 %collective-permute-start.9 = (bf16[192,512]{1,0:T(8,128)(2,1)S(1)}, bf16[192,512]{1,0:T(8,128)(2,1)S(1)}, u32[]{:S(2)}, u32[]{:S(2)}) collective-permute-start(bf16[192,512]{1,0:T(8,128)(2,1)S(1)} %pad_maximum_fusion.1), channel_id=1, source_target_pairs={{0,4},{4,0},{8,12},{12,8},{16,20},{20,16},{24,28},{28,24},{32,36},... | collective-permute-start | bytes 589832 | tf_op jit(solution)/shard_map/ppermute | solution.py:537
  22.7 0.4 collective-permute-start.8
  23.1 1.4 %project_near.1.acc = f32[4,384,160]{2,1,0:T(8,128)S(1)} custom-call(f32[4,384,160]{2,1,0:T(8,128)S(1)} %project_own.1.acc_in, bf16[384,640]{1,0:T(8,128)(2,1)S(1)} %collective-permute-done.left, bf16[384,640]{1,0:T(8,128)(2,1)S(1)} %collective-permute-done.1.right, bf16[4,640,640]{2,1,0:T(8,128)(2,1)S(1)} %get-tuple-element.44.wt), custom_call_target="tpu_custom_call" | custom-call | tf_op jit(solution)/shard_map/project_near/pallas_call | solution.py:510
  24.5 3.0 %segment_forward.1 = (bf16[3,384,768]{2,1,0:T(8,128)(2,1)S(1)}, f32[192,256]{1,0:T(8,128)S(1)}, f32[144,256]{1,0:T(8,128)S(1)}, bf16[2,192,384]{2,1,0:T(8,128)(2...) custom-call(s32[5]{0:T(128)S(1)} %stack.23.info, ...), custom_call_target="tpu_custom_call" | custom-call | tf_op jit(solution)/shard_map/segment_forward/pallas_call | solution.py:510
  27.5 0.9 %finish_low.1.g23_ref.own = bf16[144,256]{1,0:T(8,128)(2,1)S(1)} custom-call(bf16[2,336,384]{2,1,0:T(8,128)(2,1)S(1)} %get-tuple-element.42.picks, f32[4,384,160]{2,1,0:T(8,128)S(1)} %project_near.1.acc, bf16[192,640]{1,0:T(8,128)(2,1)S(1)} %collective-permute-done.5.far1, bf16[192,640]{1,0:T(8,128)(2,1)S(1)} %collective-permute-done.6.far2, ...), custom_call_target="tpu_custom_call" | custom-call | tf_op jit(solution)/shard_map/finish_low/pallas_call | solution.py:510
  28.4 1.7 %collective-permute-start.10 = (bf16[144,256]{1,0:T(8,128)(2,1)S(1)}, bf16[144,256]{1,0:T(8,128)(2,1)S(1)}, u32[]{:S(2)}, u32[]{:S(2)}) collective-permute-start(bf16[144,256]{1,0:T(8,128)(2,1)S(1)} %finish_low.1.g23_ref.own), channel_id=1, source_target_pairs={{0,8},{4,12},{8,0},{12,4},{16,24},{20,28},{24,16},{28,20},{32,40},... | collective-permute-start | bytes 221192 | tf_op jit(solution)/shard_map/ppermute | solution.py:537
  30.2 2.2 %collective-permute-start.12 = (bf16[48,256]{1,0:T(8,128)(2,1)S(1)}, bf16[48,256]{1,0:T(8,128)(2,1)S(1)}, u32[]{:S(2)}, u32[]{:S(2)}) collective-permute-start(bf16[48,256]{1,0:T(8,128)(2,1)S(1)} %slice.20), channel_id=1, source_target_pairs={{0,24},{4,28},{8,16},{12,20},{16,8},{20,12},{24,0},{28,4},{32,56},... | collective-permute-start | bytes 73736 | tf_op jit(solution)/shard_map/ppermute | solution.py:537
  32.4 1.1 %collective-permute-start.11 = (bf16[48,256]{1,0:T(8,128)(2,1)S(1)}, bf16[48,256]{1,0:T(8,128)(2,1)S(1)}, u32[]{:S(2)}, u32[]{:S(2)}) collective-permute-start(bf16[48,256]{1,0:T(8,128)(2,1)S(1)} %slice.20), channel_id=1, source_target_pairs={{0,16},{4,20},{8,24},{12,28},{16,0},{20,4},{24,8},{28,12},{32,48},... | collective-permute-start | bytes 73736 | tf_op jit(solution)/shard_map/ppermute | solution.py:537
  33.5 0.9 %finish_high.1 = (bf16[384,256]{1,0:T(8,128)(2,1)S(1)}, bf16[192,256]{1,0:T(8,128)(2,1)S(1)}) custom-call(bf16[2,336,384]{2,1,0:T(8,128)(2,1)S(1)} %get-tuple-element.42.picks, f32[4,384,160]{2,1,0:T(8,128)S(1)} %project_near.1.acc, bf16[192,640]{1,0:T(8,128)(2,1)S(1)} %collective-permute-done.5.far1, bf16[192,640]{1,0:T(8,128)(2,1)S(1)} %collective-permute-done.6.far2, ...), custom_call_target="tpu_custom_call" | custom-call | tf_op jit(solution)/shard_map/finish_high/pallas_call | solution.py:510
  34.4 0.9 %own_backward.1.d_ref = bf16[384,768]{1,0:T(8,128)(2,1)S(1)} custom-call(bf16[384,768]{1,0:T(8,128)(2,1)S(1)} %get-tuple-element.40.s0_ref, bf16[2,384,384]{2,1,0:T(8,128)(2,1)S(1)} %get-tuple-element.41.p_ref, bf16[384,256]{1,0:T(8,128)(2,1)S(1)} %get-tuple-element.59.g_ref), custom_call_target="tpu_custom_call" | custom-call | tf_op jit(solution)/shard_map/own_backward/pallas_call | solution.py:510
  35.3 1.3 %collective-permute-done.11.r4 = bf16[48,256]{1,0:T(8,128)(2,1)S(1)} collective-permute-done((bf16[48,256]{1,0:T(8,128)(2,1)S(1)}, bf16[48,256]{1,0:T(8,128)(2,1)S(1)}, u32[]{:S(2)}, u32[]{:S(2)}) %collective-permute-start.11) | collective-permute-done | bytes 24608 | tf_op jit(solution)/shard_map/ppermute | solution.py:537
  36.6 2.0 %collective-permute-start.14 = (bf16[384,256]{1,0:T(8,128)(2,1)S(1)}, bf16[384,256]{1,0:T(8,128)(2,1)S(1)}, u32[]{:S(2)}, u32[]{:S(2)}) collective-permute-start(bf16[384,256]{1,0:T(8,128)(2,1)S(1)} %pad_maximum_fusion.2), channel_id=1, source_target_pairs={{0,4},{4,0},{8,12},{12,8},{16,20},{20,16},{24,28},{28,24},{32,36},... | collective-permute-start | bytes 589832 | tf_op jit(solution)/shard_map/ppermute | solution.py:537
  38.7 1.1 %query_side.1.query_in = bf16[384,640]{1,0:T(8,128)(2,1)S(1)} custom-call(bf16[2,384,336]{2,1,0:T(8,128)(2,1)S(1)} %get-tuple-element.39.spreads, bf16[384,768]{1,0:T(8,128)(2,1)S(1)} %own_backward.1.d_ref, bf16[3,384,768]{2,1,0:T(8,128)(2,1)S(1)} %get-tuple-element.63.f_ref, bf16[192,256]{1,0:T(8,128)(2,1)S(1)} %get-tuple-element.64.g1_ref.own, ...), custom_call_target="tpu_custom_call" | custom-call | tf_op jit(solution)/shard_map/query_side/pallas_call | solution.py:510
  40.0 1.0 %key_value_high.1 = (bf16[384,640]{1,0:T(8,128)(2,1)S(1)}, bf16[384,640]{1,0:T(8,128)(2,1)S(1)}) custom-call(bf16[2,384,336]{2,1,0:T(8,128)(2,1)S(1)} %get-tuple-element.39.spreads, bf16[384,768]{1,0:T(8,128)(2,1)S(1)} %own_backward.1.d_ref, bf16[3,384,768]{2,1,0:T(8,128)(2,1)S(1)} %get-tuple-element.63.f_ref, ...), custom_call_target="tpu_custom_call" | custom-call | tf_op jit(solution)/shard_map/key_value_high/pallas_call | solution.py:510
  41.0 1.9 %key_value_low.1 = (bf16[384,640]{1,0:T(8,128)(2,1)}, bf16[384,640]{1,0:T(8,128)(2,1)}, bf16[384,640]{1,0:T(8,128)(2,1)}) custom-call(bf16[2,384,336]{2,1,0:T(8,128)(2,1)S(1)} %get-tuple-element.39.spreads, bf16[384,640]{1,0:T(8,128)(2,1)S(1)} %query_side.1.query_in, bf16[384,640]{1,0:T(8,128)(2,1)S(1)} %get-tuple-element.69.key_in, ...), custom_call_target="tpu_custom_call" | custom-call | tf_op jit(solution)/shard_map/key_value_low/pallas_call | solution.py:510
  (26 shorter events, 0.6 us)
Async XLA Ops:
  0.6 13.9 %collective-permute-start.1 = (bf16[384,640]{1,0:T(8,128)(2,1)}, bf16[384,640]{1,0:T(8,128)(2,1)S(1)}, u32[]{:S(2)}, u32[]{:S(2)}) collective-permute-start(bf16[384,640]{1,0:T(8,128)(2,1)} %og_hbm.1), channel_id=1, source_target_pairs={{0,3},{1,0},{2,1},{3,2},{4,7},{5,4},{6,5},{7,6},{8,11},{9,8},{10,9... | collective-permute-start | bytes 1474568 | tf_op jit(solution)/shard_map/ppermute | solution.py:547
  4.0 13.2 %collective-permute-start = (bf16[384,640]{1,0:T(8,128)(2,1)}, bf16[384,640]{1,0:T(8,128)(2,1)S(1)}, u32[]{:S(2)}, u32[]{:S(2)}) collective-permute-start(bf16[384,640]{1,0:T(8,128)(2,1)} %og_hbm.1), channel_id=1, source_target_pairs={{0,1},{1,2},{2,3},{3,0},{4,5},{5,6},{6,7},{7,4},{8,9},{9,10},{10,1... | collective-permute-start | bytes 1474568 | tf_op jit(solution)/shard_map/ppermute | solution.py:546
  7.2 10.0 %collective-permute-start.2 = (bf16[144,512]{1,0:T(8,128)(2,1)S(1)}, bf16[144,512]{1,0:T(8,128)(2,1)S(1)}, u32[]{:S(2)}, u32[]{:S(2)}) collective-permute-start(bf16[144,512]{1,0:T(8,128)(2,1)S(1)} %get-tuple-element.47), channel_id=1, source_target_pairs={{0,8},{4,12},{8,0},{12,4},{16,24},{20,28},{24,16},{28,20},{32,40},... | collective-permute-start | bytes 442376 | tf_op jit(solution)/shard_map/ppermute | solution.py:537
  8.9 8.3 %collective-permute-start.4 = (bf16[48,512]{1,0:T(8,128)(2,1)S(1)}, bf16[48,512]{1,0:T(8,128)(2,1)S(1)}, u32[]{:S(2)}, u32[]{:S(2)}) collective-permute-start(bf16[48,512]{1,0:T(8,128)(2,1)S(1)} %slice.15), channel_id=1, source_target_pairs={{0,24},{4,28},{8,16},{12,20},{16,8},{20,12},{24,0},{28,4},{32,56},... | collective-permute-start | bytes 147464 | tf_op jit(solution)/shard_map/ppermute | solution.py:537
  11.2 6.0 %collective-permute-start.3 = (bf16[48,512]{1,0:T(8,128)(2,1)S(1)}, bf16[48,512]{1,0:T(8,128)(2,1)S(1)}, u32[]{:S(2)}, u32[]{:S(2)}) collective-permute-start(bf16[48,512]{1,0:T(8,128)(2,1)S(1)} %slice.15), channel_id=1, source_target_pairs={{0,16},{4,20},{8,24},{12,28},{16,0},{20,4},{24,8},{28,12},{32,48},... | collective-permute-start | bytes 147464 | tf_op jit(solution)/shard_map/ppermute | solution.py:537
  17.3 10.2 %collective-permute-start.5 = (bf16[192,640]{1,0:T(8,128)(2,1)S(1)}, bf16[192,640]{1,0:T(8,128)(2,1)S(1)}, u32[]{:S(2)}, u32[]{:S(2)}) collective-permute-start(bf16[192,640]{1,0:T(8,128)(2,1)S(1)} %slice.16), channel_id=1, source_target_pairs={{0,1},{1,2},{2,3},{3,0},{4,5},{5,6},{6,7},{7,4},{8,9},{9,10},{10,1... | collective-permute-start | bytes 737288 | tf_op jit(solution)/shard_map/ppermute | solution.py:590
  17.4 10.1 %collective-permute-start.6 = (bf16[192,640]{1,0:T(8,128)(2,1)S(1)}, bf16[192,640]{1,0:T(8,128)(2,1)S(1)}, u32[]{:S(2)}, u32[]{:S(2)}) collective-permute-start(bf16[192,640]{1,0:T(8,128)(2,1)S(1)} %slice.17), channel_id=1, source_target_pairs={{0,3},{1,0},{2,1},{3,2},{4,7},{5,4},{6,5},{7,6},{8,11},{9,8},{10,9... | collective-permute-start | bytes 737288 | tf_op jit(solution)/shard_map/ppermute | solution.py:591
  20.1 4.4 %collective-permute-start.9 = (bf16[192,512]{1,0:T(8,128)(2,1)S(1)}, bf16[192,512]{1,0:T(8,128)(2,1)S(1)}, u32[]{:S(2)}, u32[]{:S(2)}) collective-permute-start(bf16[192,512]{1,0:T(8,128)(2,1)S(1)} %pad_maximum_fusion.1), channel_id=1, source_target_pairs={{0,4},{4,0},{8,12},{12,8},{16,20},{20,16},{24,28},{28,24},{32,36},... | collective-permute-start | bytes 589832 | tf_op jit(solution)/shard_map/ppermute | solution.py:537
  22.6 1.9 %collective-permute-start.7 = (bf16[192,512]{1,0:T(8,128)(2,1)S(1)}, bf16[192,512]{1,0:T(8,128)(2,1)S(1)}, u32[]{:S(2)}, u32[]{:S(2)}) collective-permute-start(bf16[192,512]{1,0:T(8,128)(2,1)S(1)} %slice.18), channel_id=1, source_target_pairs={{0,4},{4,0},{8,12},{12,8},{16,20},{20,16},{24,28},{28,24},{32,36},... | collective-permute-start | bytes 589832 | tf_op jit(solution)/shard_map/ppermute | solution.py:537
  22.7 1.8 %collective-permute-start.8 = (bf16[192,512]{1,0:T(8,128)(2,1)S(1)}, bf16[192,512]{1,0:T(8,128)(2,1)S(1)}, u32[]{:S(2)}, u32[]{:S(2)}) collective-permute-start(bf16[192,512]{1,0:T(8,128)(2,1)S(1)} %pad_maximum_fusion), channel_id=1, source_target_pairs={{0,4},{4,0},{8,12},{12,8},{16,20},{20,16},{24,28},{28,24},{32,36},... | collective-permute-start | bytes 589832 | tf_op jit(solution)/shard_map/ppermute | solution.py:537
  28.4 8.2 %collective-permute-start.10 = (bf16[144,256]{1,0:T(8,128)(2,1)S(1)}, bf16[144,256]{1,0:T(8,128)(2,1)S(1)}, u32[]{:S(2)}, u32[]{:S(2)}) collective-permute-start(bf16[144,256]{1,0:T(8,128)(2,1)S(1)} %finish_low.1.g23_ref.own), channel_id=1, source_target_pairs={{0,8},{4,12},{8,0},{12,4},{16,24},{20,28},{24,16},{28,20},{32,40},... | collective-permute-start | bytes 221192 | tf_op jit(solution)/shard_map/ppermute | solution.py:537
  30.2 5.1 %collective-permute-start.12 = (bf16[48,256]{1,0:T(8,128)(2,1)S(1)}, bf16[48,256]{1,0:T(8,128)(2,1)S(1)}, u32[]{:S(2)}, u32[]{:S(2)}) collective-permute-start(bf16[48,256]{1,0:T(8,128)(2,1)S(1)} %slice.20), channel_id=1, source_target_pairs={{0,24},{4,28},{8,16},{12,20},{16,8},{20,12},{24,0},{28,4},{32,56},... | collective-permute-start | bytes 73736 | tf_op jit(solution)/shard_map/ppermute | solution.py:537
  32.4 4.2 %collective-permute-start.11 = (bf16[48,256]{1,0:T(8,128)(2,1)S(1)}, bf16[48,256]{1,0:T(8,128)(2,1)S(1)}, u32[]{:S(2)}, u32[]{:S(2)}) collective-permute-start(bf16[48,256]{1,0:T(8,128)(2,1)S(1)} %slice.20), channel_id=1, source_target_pairs={{0,16},{4,20},{8,24},{12,28},{16,0},{20,4},{24,8},{28,12},{32,48},... | collective-permute-start | bytes 73736 | tf_op jit(solution)/shard_map/ppermute | solution.py:537
  36.6 4.3 %collective-permute-start.14 = (bf16[384,256]{1,0:T(8,128)(2,1)S(1)}, bf16[384,256]{1,0:T(8,128)(2,1)S(1)}, u32[]{:S(2)}, u32[]{:S(2)}) collective-permute-start(bf16[384,256]{1,0:T(8,128)(2,1)S(1)} %pad_maximum_fusion.2), channel_id=1, source_target_pairs={{0,4},{4,0},{8,12},{12,8},{16,20},{20,16},{24,28},{28,24},{32,36},... | collective-permute-start | bytes 589832 | tf_op jit(solution)/shard_map/ppermute | solution.py:537
  38.7 1.3 %collective-permute-start.13 = (bf16[192,256]{1,0:T(8,128)(2,1)S(1)}, bf16[192,256]{1,0:T(8,128)(2,1)S(1)}, u32[]{:S(2)}, u32[]{:S(2)}) collective-permute-start(bf16[192,256]{1,0:T(8,128)(2,1)S(1)} %get-tuple-element.64.g1_ref.own), channel_id=1, source_target_pairs={{0,4},{4,0},{8,12},{12,8},{16,20},{20,16},{24,28},{28,24},{32,36},... | collective-permute-start | bytes 294920 | tf_op jit(solution)/shard_map/ppermute | solution.py:537

commit v2 on v1

--- a/solution.py
+++ b/solution.py
@@ -396,21 +396,6 @@
     store_halves(out_ref, halves)
 
 
-def key_value_high_kernel(spreads, d_ref, f_ref, own, near, pk, key_ref, value_ref, g_scr, b_scr):
-    tok = key_ref.shape[0]
-    n = tok // 2
-    g_scr[:n] = own[...]
-    g_scr[n:] = near[...]
-    key_value_rows((1,), tok, f_ref, (g_scr,), {1: pk}, b_scr)
-    for i, out_ref in enumerate((key_ref, value_ref)):
-        parts = []
-        for a in range(2):
-            c = (i + 1) * PAIR + a * SLOT
-            x = dot(spreads[a, :, :n], b_scr[i, a], NN)
-            parts.append(add_own(x, a, d_ref[:, c : c + SLOT]))
-        store_halves(out_ref, parts)
-
-
 def key_value_rows(groups, tok, f_ref, g_scr, pks, b_scr):
     rows, first = starts_of(tok)
     chain = [(g, a) for g in groups for a in range(2)]
@@ -430,17 +415,18 @@
         place_rows(b_scr.at[1, a], at, g, a, clear(dot(pks[g][a], gg, NN)))
 
 
-def key_value_low_kernel(
+def key_value_kernel(
     spreads,
     query_in,
-    key_in,
-    value_in,
+    d_ref,
     f_ref,
+    own1,
     own,
     r2,
     r4,
     r6,
     d,
+    k1,
     k2,
     k3,
     query_out,
@@ -453,7 +439,7 @@
     sems,
 ):
     tok = key_scr.shape[0]
-    n = tok // 2
+    n, low = own1.shape[0], own.shape[0]
     copies = [
         pltpu.make_async_copy(x, out, sems.at[i])
         for i, (x, out) in enumerate(
@@ -461,26 +447,32 @@
         )
     ]
     copies[0].start()
-    for g in (2, 3):
-        m, low = tok >> g, r2.shape[0]
-        parts = parts_of(
-            g,
-            tok,
-            (own, 0),
-            (d, 0),
-            (r2, 0),
-            (d, low),
-            (r4, 0),
-            (r6, 0),
-            (d, 2 * low),
-            (d, 2 * low + r4.shape[0]),
-        )
+    for g in (1, 2, 3):
+        m = tok >> g
+        parts = [(own1, 0), (d, 0)]
+        if g > 1:
+            parts = parts_of(
+                g,
+                tok,
+                (own, 0),
+                (d, n),
+                (r2, 0),
+                (d, n + low),
+                (r4, 0),
+                (r6, 0),
+                (d, n + 2 * low),
+                (d, n + 2 * low + r4.shape[0]),
+            )
         for i, (ref, at) in enumerate(parts):
-            g_scr[g - 2, i * m : (i + 1) * m, :] = ref[at : at + m, :]
-    key_value_rows((2, 3), tok, f_ref, (g_scr.at[0], g_scr.at[1]), {2: k2, 3: k3}, b_scr)
-    for i, (base, out) in enumerate(((key_in, key_scr), (value_in, value_scr))):
-        parts = [dot(spreads[a, :, n:], b_scr[i, a], NN) for a in range(2)]
-        store_halves(out, parts, base)
+            g_scr[g - 1, i * m : (i + 1) * m, :] = ref[at : at + m, :]
+    g_refs = tuple(g_scr.at[i] for i in range(3))
+    key_value_rows((1, 2, 3), tok, f_ref, g_refs, {1: k1, 2: k2, 3: k3}, b_scr)
+    for i, out in enumerate((key_scr, value_scr)):
+        parts = []
+        for a in range(2):
+            c = (i + 1) * PAIR + a * SLOT
+            parts.append(add_own(dot(spreads[a], b_scr[i, a], NN), a, d_ref[:, c : c + SLOT]))
+        store_halves(out, parts)
         copies[i + 1].start()
     for copy in copies:
         copy.wait()
@@ -626,7 +618,6 @@
         scratches=pair_scratch,
         name="finish_high",
     )
-    g_near = swap(g1, 1)
     d0 = call(
         own_backward_kernel,
         shape(tok, 3 * PAIR),
@@ -634,38 +625,31 @@
         scratches=(scratch(2, tok, tok),),
         name="own_backward",
     )
-    g_far = lax.optimization_barrier(g_far + (d0,))[:3]
-    g_d = swap(jnp.concatenate((g23,) + g_far, 0), 1)
-    key_part, value_part = call(
-        key_value_high_kernel,
-        (shape(tok, width), shape(tok, width)),
-        (spreads, after(d0, g_far[1]), full, g1, g_near, pk[0]),
-        scratches=(scratch(tok, PAIR), scratch(2, 2, rows[1], 3 * SLOT)),
-        name="key_value_high",
-    )
     query_part = call(
         query_kernel,
         shape(tok, width),
-        (spreads, after(d0, g_far[1]), full, g1, g23) + tuple(pq),
+        (spreads, d0, full, g1, g23) + tuple(pq),
         scratches=(scratch(2, n_all, 3 * SLOT),),
         name="query_side",
     )
+    g_far = lax.optimization_barrier(g_far + (query_part,))[:3]
+    g_d = swap(jnp.concatenate((g1, g23) + g_far, 0), 1)
     return tuple(
         call(
-            key_value_low_kernel,
+            key_value_kernel,
             (shape(tok, width),) * 3,
-            (spreads, query_part, key_part, value_part, full, g23)
+            (spreads, query_part, d0, full, g1, g23)
             + g_far
             + (g_d,)
-            + tuple(pk[1:]),
+            + tuple(pk),
             scratches=(
-                scratch(2, tok, PAIR),
-                scratch(2, 2, n_low, 3 * SLOT),
+                scratch(3, tok, PAIR),
+                scratch(2, 2, n_all, 3 * SLOT),
                 scratch(tok, width),
                 scratch(tok, width),
                 dma((3,)),
             ),
-            name="key_value_low",
+            name="key_value",
             out=HB,
         )
     )

time: 43.1 us -> 42.2 us (0.979)
  starting transfers between devices: 21.4 us -> 20.6 us
  Pallas kernels: 16.4 us -> 15.9 us
    ppermute x11 -> x10, starting transfers between devices: 15.3 us -> 14.5 us  [swap(): return lax.ppermute(x, 'seq', [(i, i ^ mask) for i in range(n_seq)])]
    pallas_call x11 -> x10, Pallas kernels: 16.4 us -> 15.9 us  [call(): pl.pallas_call(kernel, out_shape=outs, in_specs=specs, out_specs=jax.tree...]
    ppermute x11 -> x10, waiting for transfers between devices: 1.4 us -> 1.76 us  [swap(): return lax.ppermute(x, 'seq', [(i, i ^ mask) for i in range(n_seq)])]
  transfers between devices with their start and end apart: 15 -> 14, of which waited for: 3 -> 3; matrix products, arithmetic and copies ran while one was open for 0% -> 0% of each run, Pallas kernels for 32% -> 30%
where the time goes in v2:
time: 42.2 us; the launch traced here: 42.1 us
  starting transfers between devices  20.6 us (49%)
  Pallas kernels  15.9 us (38%)
  waiting for transfers between devices  4.41 us (10%)
  between operations  1.01 us (2%)
    pallas_call x10, Pallas kernels, call(): pl.pallas_call(kernel, out_shape=outs, in_specs=specs, out_specs=jax.tree...  15.9 us
    ppermute x10, starting transfers between devices, swap(): return lax.ppermute(x, 'seq', [(i, i ^ mask) for i in range(n_seq)])  14.5 us
    ppermute x1, starting transfers between devices, on_device(): right = lax.ppermute(out_grad, 'head', left_way)  3.38 us
    ppermute x1, starting transfers between devices, on_device(): far2 = lax.ppermute(right[half:], 'head', left_way)  2.66 us
    ppermute x1, waiting for transfers between devices, on_device(): left = lax.ppermute(out_grad, 'head', right_way)  2.65 us
    ppermute x10, waiting for transfers between devices, swap(): return lax.ppermute(x, 'seq', [(i, i ^ mask) for i in range(n_seq)])  1.76 us
  transfers between devices with their start and end apart: 14, of which 3 were waited for; matrix products, arithmetic and copies ran while one was open for 0% of the time, Pallas kernels for 30%

profile of v2, /device:TPU:1, one launch (start us, length us, event | category | flops | bytes accessed | tf_op | source)
XLA Modules:
  0.0 42.1 jit_solution(3503829156034905045)
XLA Ops:
  0.6 3.4 %collective-permute-start.1 = (bf16[384,640]{1,0:T(8,128)(2,1)}, bf16[384,640]{1,0:T(8,128)(2,1)S(1)}, u32[]{:S(2)}, u32[]{:S(2)}) collective-permute-start(bf16[384,640]{1,0:T(8,128)(2,1)} %og_hbm.1), channel_id=1, source_target_pairs={{0,3},{1,0},{2,1},{3,2},{4,7},{5,4},{6,5},{7,6},{8,11},{9,8},{10,9... | collective-permute-start | bytes 1474568 | tf_op jit(solution)/shard_map/ppermute | solution.py:539
  4.1 3.1 %select.7 = (bf16[384,768]{1,0:T(8,128)(2,1)S(1)}, bf16[336,512]{1,0:T(8,128)(2,1)S(1)}, bf16[144,512]{1,0:T(8,128)(2,1)S(1)}, bf16[2,336,384]{2,1,0:T(8,128)(2,...) custom-call(s32[5]{0:T(128)S(1)} %stack.23.info, ...), custom_call_target="tpu_custom_call" | custom-call | tf_op jit(solution)/shard_map/select/pallas_call | solution.py:502
  7.2 1.7 %collective-permute-start.2 = (bf16[144,512]{1,0:T(8,128)(2,1)S(1)}, bf16[144,512]{1,0:T(8,128)(2,1)S(1)}, u32[]{:S(2)}, u32[]{:S(2)}) collective-permute-start(bf16[144,512]{1,0:T(8,128)(2,1)S(1)} %get-tuple-element.44), channel_id=1, source_target_pairs={{0,8},{4,12},{8,0},{12,4},{16,24},{20,28},{24,16},{28,20},{32,40},... | collective-permute-start | bytes 442376 | tf_op jit(solution)/shard_map/ppermute | solution.py:529
  8.9 2.2 %collective-permute-start.4 = (bf16[48,512]{1,0:T(8,128)(2,1)S(1)}, bf16[48,512]{1,0:T(8,128)(2,1)S(1)}, u32[]{:S(2)}, u32[]{:S(2)}) collective-permute-start(bf16[48,512]{1,0:T(8,128)(2,1)S(1)} %slice.15), channel_id=1, source_target_pairs={{0,24},{4,28},{8,16},{12,20},{16,8},{20,12},{24,0},{28,4},{32,56},... | collective-permute-start | bytes 147464 | tf_op jit(solution)/shard_map/ppermute | solution.py:529
  11.2 1.1 %collective-permute-start.3 = (bf16[48,512]{1,0:T(8,128)(2,1)S(1)}, bf16[48,512]{1,0:T(8,128)(2,1)S(1)}, u32[]{:S(2)}, u32[]{:S(2)}) collective-permute-start(bf16[48,512]{1,0:T(8,128)(2,1)S(1)} %slice.15), channel_id=1, source_target_pairs={{0,16},{4,20},{8,24},{12,28},{16,0},{20,4},{24,8},{28,12},{32,48},... | collective-permute-start | bytes 147464 | tf_op jit(solution)/shard_map/ppermute | solution.py:529
  12.3 1.4 %own_forward.1 = (bf16[2,384,384]{2,1,0:T(8,128)(2,1)S(1)}, f32[384,256]{1,0:T(8,128)S(1)}) custom-call(bf16[384,768]{1,0:T(8,128)(2,1)S(1)} %get-tuple-element.37.s0_ref), custom_call_target="tpu_custom_call" | custom-call | tf_op jit(solution)/shard_map/own_forward/pallas_call | solution.py:502
  13.8 0.8 %project_own.1.acc_in = f32[4,384,160]{2,1,0:T(8,128)S(1)} custom-call(bf16[384,640]{1,0:T(8,128)(2,1)S(1)} %get-tuple-element.40.own, bf16[4,640,640]{2,1,0:T(8,128)(2,1)S(1)} %get-tuple-element.41.wt), custom_call_target="tpu_custom_call" | custom-call | tf_op jit(solution)/shard_map/project_own/pallas_call | solution.py:502
  14.6 2.6 %collective-permute-done.left = bf16[384,640]{1,0:T(8,128)(2,1)S(1)} collective-permute-done((bf16[384,640]{1,0:T(8,128)(2,1)}, bf16[384,640]{1,0:T(8,128)(2,1)S(1)}, u32[]{:S(2)}, u32[]{:S(2)}) %collective-permute-start) | collective-permute-done | bytes 491552 | tf_op jit(solution)/shard_map/ppermute | solution.py:538
  17.4 2.7 %collective-permute-start.6 = (bf16[192,640]{1,0:T(8,128)(2,1)S(1)}, bf16[192,640]{1,0:T(8,128)(2,1)S(1)}, u32[]{:S(2)}, u32[]{:S(2)}) collective-permute-start(bf16[192,640]{1,0:T(8,128)(2,1)S(1)} %slice.17), channel_id=1, source_target_pairs={{0,3},{1,0},{2,1},{3,2},{4,7},{5,4},{6,5},{7,6},{8,11},{9,8},{10,9... | collective-permute-start | bytes 737288 | tf_op jit(solution)/shard_map/ppermute | solution.py:583
  20.1 2.5 %collective-permute-start.9 = (bf16[192,512]{1,0:T(8,128)(2,1)S(1)}, bf16[192,512]{1,0:T(8,128)(2,1)S(1)}, u32[]{:S(2)}, u32[]{:S(2)}) collective-permute-start(bf16[192,512]{1,0:T(8,128)(2,1)S(1)} %pad_maximum_fusion.1), channel_id=1, source_target_pairs={{0,4},{4,0},{8,12},{12,8},{16,20},{20,16},{24,28},{28,24},{32,36},... | collective-permute-start | bytes 589832 | tf_op jit(solution)/shard_map/ppermute | solution.py:529
  22.6 0.1 collective-permute-start.7
  22.7 0.4 collective-permute-start.8
  23.1 1.4 %project_near.1.acc = f32[4,384,160]{2,1,0:T(8,128)S(1)} custom-call(f32[4,384,160]{2,1,0:T(8,128)S(1)} %project_own.1.acc_in, bf16[384,640]{1,0:T(8,128)(2,1)S(1)} %collective-permute-done.left, bf16[384,640]{1,0:T(8,128)(2,1)S(1)} %collective-permute-done.1.right, bf16[4,640,640]{2,1,0:T(8,128)(2,1)S(1)} %get-tuple-element.41.wt), custom_call_target="tpu_custom_call" | custom-call | tf_op jit(solution)/shard_map/project_near/pallas_call | solution.py:502
  24.5 3.0 %segment_forward.1 = (bf16[3,384,768]{2,1,0:T(8,128)(2,1)S(1)}, f32[192,256]{1,0:T(8,128)S(1)}, f32[144,256]{1,0:T(8,128)S(1)}, bf16[2,192,384]{2,1,0:T(8,128)(2...) custom-call(s32[5]{0:T(128)S(1)} %stack.23.info, ...), custom_call_target="tpu_custom_call" | custom-call | tf_op jit(solution)/shard_map/segment_forward/pallas_call | solution.py:502
  27.5 0.9 %finish_low.1.g23_ref.own = bf16[144,256]{1,0:T(8,128)(2,1)S(1)} custom-call(bf16[2,336,384]{2,1,0:T(8,128)(2,1)S(1)} %get-tuple-element.39.picks, f32[4,384,160]{2,1,0:T(8,128)S(1)} %project_near.1.acc, bf16[192,640]{1,0:T(8,128)(2,1)S(1)} %collective-permute-done.5.far1, bf16[192,640]{1,0:T(8,128)(2,1)S(1)} %collective-permute-done.6.far2, ...), custom_call_target="tpu_custom_call" | custom-call | tf_op jit(solution)/shard_map/finish_low/pallas_call | solution.py:502
  28.4 3.8 %collective-permute-start.12 = (bf16[48,256]{1,0:T(8,128)(2,1)S(1)}, bf16[48,256]{1,0:T(8,128)(2,1)S(1)}, u32[]{:S(2)}, u32[]{:S(2)}) collective-permute-start(bf16[48,256]{1,0:T(8,128)(2,1)S(1)} %slice.20), channel_id=1, source_target_pairs={{0,24},{4,28},{8,16},{12,20},{16,8},{20,12},{24,0},{28,4},{32,56},... | collective-permute-start | bytes 73736 | tf_op jit(solution)/shard_map/ppermute | solution.py:529
  32.3 0.7 %collective-permute-start.10 = (bf16[144,256]{1,0:T(8,128)(2,1)S(1)}, bf16[144,256]{1,0:T(8,128)(2,1)S(1)}, u32[]{:S(2)}, u32[]{:S(2)}) collective-permute-start(bf16[144,256]{1,0:T(8,128)(2,1)S(1)} %finish_low.1.g23_ref.own), channel_id=1, source_target_pairs={{0,8},{4,12},{8,0},{12,4},{16,24},{20,28},{24,16},{28,20},{32,40},... | collective-permute-start | bytes 221192 | tf_op jit(solution)/shard_map/ppermute | solution.py:529
  33.0 0.9 %finish_high.1 = (bf16[384,256]{1,0:T(8,128)(2,1)S(1)}, bf16[192,256]{1,0:T(8,128)(2,1)S(1)}) custom-call(bf16[2,336,384]{2,1,0:T(8,128)(2,1)S(1)} %get-tuple-element.39.picks, f32[4,384,160]{2,1,0:T(8,128)S(1)} %project_near.1.acc, bf16[192,640]{1,0:T(8,128)(2,1)S(1)} %collective-permute-done.5.far1, bf16[192,640]{1,0:T(8,128)(2,1)S(1)} %collective-permute-done.6.far2, ...), custom_call_target="tpu_custom_call" | custom-call | tf_op jit(solution)/shard_map/finish_high/pallas_call | solution.py:502
  33.9 0.9 %own_backward.1.d_ref = bf16[384,768]{1,0:T(8,128)(2,1)S(1)} custom-call(bf16[384,768]{1,0:T(8,128)(2,1)S(1)} %get-tuple-element.37.s0_ref, bf16[2,384,384]{2,1,0:T(8,128)(2,1)S(1)} %get-tuple-element.38.p_ref, bf16[384,256]{1,0:T(8,128)(2,1)S(1)} %get-tuple-element.56.g_ref), custom_call_target="tpu_custom_call" | custom-call | tf_op jit(solution)/shard_map/own_backward/pallas_call | solution.py:502
  34.8 1.1 %query_side.1.query_in = bf16[384,640]{1,0:T(8,128)(2,1)S(1)} custom-call(bf16[2,384,336]{2,1,0:T(8,128)(2,1)S(1)} %get-tuple-element.36.spreads, bf16[384,768]{1,0:T(8,128)(2,1)S(1)} %own_backward.1.d_ref, bf16[3,384,768]{2,1,0:T(8,128)(2,1)S(1)} %get-tuple-element.57.f_ref, bf16[192,256]{1,0:T(8,128)(2,1)S(1)} %get-tuple-element.58.g1_ref.own1, ...), custom_call_target="tpu_custom_call" | custom-call | tf_op jit(solution)/shard_map/query_side/pallas_call | solution.py:502
  35.9 0.5 %collective-permute-done.11.r4 = bf16[48,256]{1,0:T(8,128)(2,1)S(1)} collective-permute-done((bf16[48,256]{1,0:T(8,128)(2,1)S(1)}, bf16[48,256]{1,0:T(8,128)(2,1)S(1)}, u32[]{:S(2)}, u32[]{:S(2)}) %collective-permute-start.11) | collective-permute-done | bytes 24608 | tf_op jit(solution)/shard_map/ppermute | solution.py:529
  36.5 1.8 %collective-permute-start.13 = (bf16[576,256]{1,0:T(8,128)(2,1)S(1)}, bf16[576,256]{1,0:T(8,128)(2,1)S(1)}, u32[]{:S(2)}, u32[]{:S(2)}) collective-permute-start(bf16[576,256]{1,0:T(8,128)(2,1)S(1)} %constant_dynamic-update-slice_fusion), channel_id=1, source_target_pairs={{0,4},{4,0},{8,12},{12,8},{16,20},{20,16},{24,28},{28,24},{32,36},... | collective-permute-start | bytes 884744 | tf_op jit(solution)/shard_map/ppermute | solution.py:529
  38.3 1.2 %collective-permute-done.13.d = bf16[576,256]{1,0:T(8,128)(2,1)S(1)} collective-permute-done((bf16[576,256]{1,0:T(8,128)(2,1)S(1)}, bf16[576,256]{1,0:T(8,128)(2,1)S(1)}, u32[]{:S(2)}, u32[]{:S(2)}) %collective-permute-start.13) | collective-permute-done | bytes 294944 | tf_op jit(solution)/shard_map/ppermute | solution.py:529
  39.5 2.4 %key_value.1 = (bf16[384,640]{1,0:T(8,128)(2,1)}, bf16[384,640]{1,0:T(8,128)(2,1)}, bf16[384,640]{1,0:T(8,128)(2,1)}) custom-call(bf16[2,384,336]{2,1,0:T(8,128)(2,1)S(1)} %get-tuple-element.36.spreads, bf16[384,640]{1,0:T(8,128)(2,1)S(1)} %query_side.1.query_in, bf16[384,768]{1,0:T(8,128)(2,1)S(1)} %own_backward.1.d_ref, ...), custom_call_target="tpu_custom_call" | custom-call | tf_op jit(solution)/shard_map/key_value/pallas_call | solution.py:502
  (27 shorter events, 0.3 us)
Async XLA Ops:
  0.6 13.9 %collective-permute-start.1 = (bf16[384,640]{1,0:T(8,128)(2,1)}, bf16[384,640]{1,0:T(8,128)(2,1)S(1)}, u32[]{:S(2)}, u32[]{:S(2)}) collective-permute-start(bf16[384,640]{1,0:T(8,128)(2,1)} %og_hbm.1), channel_id=1, source_target_pairs={{0,3},{1,0},{2,1},{3,2},{4,7},{5,4},{6,5},{7,6},{8,11},{9,8},{10,9... | collective-permute-start | bytes 1474568 | tf_op jit(solution)/shard_map/ppermute | solution.py:539
  4.0 13.2 %collective-permute-start = (bf16[384,640]{1,0:T(8,128)(2,1)}, bf16[384,640]{1,0:T(8,128)(2,1)S(1)}, u32[]{:S(2)}, u32[]{:S(2)}) collective-permute-start(bf16[384,640]{1,0:T(8,128)(2,1)} %og_hbm.1), channel_id=1, source_target_pairs={{0,1},{1,2},{2,3},{3,0},{4,5},{5,6},{6,7},{7,4},{8,9},{9,10},{10,1... | collective-permute-start | bytes 1474568 | tf_op jit(solution)/shard_map/ppermute | solution.py:538
  7.2 10.0 %collective-permute-start.2 = (bf16[144,512]{1,0:T(8,128)(2,1)S(1)}, bf16[144,512]{1,0:T(8,128)(2,1)S(1)}, u32[]{:S(2)}, u32[]{:S(2)}) collective-permute-start(bf16[144,512]{1,0:T(8,128)(2,1)S(1)} %get-tuple-element.44), channel_id=1, source_target_pairs={{0,8},{4,12},{8,0},{12,4},{16,24},{20,28},{24,16},{28,20},{32,40},... | collective-permute-start | bytes 442376 | tf_op jit(solution)/shard_map/ppermute | solution.py:529
  8.9 8.3 %collective-permute-start.4 = (bf16[48,512]{1,0:T(8,128)(2,1)S(1)}, bf16[48,512]{1,0:T(8,128)(2,1)S(1)}, u32[]{:S(2)}, u32[]{:S(2)}) collective-permute-start(bf16[48,512]{1,0:T(8,128)(2,1)S(1)} %slice.15), channel_id=1, source_target_pairs={{0,24},{4,28},{8,16},{12,20},{16,8},{20,12},{24,0},{28,4},{32,56},... | collective-permute-start | bytes 147464 | tf_op jit(solution)/shard_map/ppermute | solution.py:529
  11.2 6.0 %collective-permute-start.3 = (bf16[48,512]{1,0:T(8,128)(2,1)S(1)}, bf16[48,512]{1,0:T(8,128)(2,1)S(1)}, u32[]{:S(2)}, u32[]{:S(2)}) collective-permute-start(bf16[48,512]{1,0:T(8,128)(2,1)S(1)} %slice.15), channel_id=1, source_target_pairs={{0,16},{4,20},{8,24},{12,28},{16,0},{20,4},{24,8},{28,12},{32,48},... | collective-permute-start | bytes 147464 | tf_op jit(solution)/shard_map/ppermute | solution.py:529
  17.3 10.2 %collective-permute-start.5 = (bf16[192,640]{1,0:T(8,128)(2,1)S(1)}, bf16[192,640]{1,0:T(8,128)(2,1)S(1)}, u32[]{:S(2)}, u32[]{:S(2)}) collective-permute-start(bf16[192,640]{1,0:T(8,128)(2,1)S(1)} %slice.16), channel_id=1, source_target_pairs={{0,1},{1,2},{2,3},{3,0},{4,5},{5,6},{6,7},{7,4},{8,9},{9,10},{10,1... | collective-permute-start | bytes 737288 | tf_op jit(solution)/shard_map/ppermute | solution.py:582
  17.4 10.1 %collective-permute-start.6 = (bf16[192,640]{1,0:T(8,128)(2,1)S(1)}, bf16[192,640]{1,0:T(8,128)(2,1)S(1)}, u32[]{:S(2)}, u32[]{:S(2)}) collective-permute-start(bf16[192,640]{1,0:T(8,128)(2,1)S(1)} %slice.17), channel_id=1, source_target_pairs={{0,3},{1,0},{2,1},{3,2},{4,7},{5,4},{6,5},{7,6},{8,11},{9,8},{10,9... | collective-permute-start | bytes 737288 | tf_op jit(solution)/shard_map/ppermute | solution.py:583
  20.1 4.4 %collective-permute-start.9 = (bf16[192,512]{1,0:T(8,128)(2,1)S(1)}, bf16[192,512]{1,0:T(8,128)(2,1)S(1)}, u32[]{:S(2)}, u32[]{:S(2)}) collective-permute-start(bf16[192,512]{1,0:T(8,128)(2,1)S(1)} %pad_maximum_fusion.1), channel_id=1, source_target_pairs={{0,4},{4,0},{8,12},{12,8},{16,20},{20,16},{24,28},{28,24},{32,36},... | collective-permute-start | bytes 589832 | tf_op jit(solution)/shard_map/ppermute | solution.py:529
  22.6 1.9 %collective-permute-start.7 = (bf16[192,512]{1,0:T(8,128)(2,1)S(1)}, bf16[192,512]{1,0:T(8,128)(2,1)S(1)}, u32[]{:S(2)}, u32[]{:S(2)}) collective-permute-start(bf16[192,512]{1,0:T(8,128)(2,1)S(1)} %slice.18), channel_id=1, source_target_pairs={{0,4},{4,0},{8,12},{12,8},{16,20},{20,16},{24,28},{28,24},{32,36},... | collective-permute-start | bytes 589832 | tf_op jit(solution)/shard_map/ppermute | solution.py:529
  22.7 1.8 %collective-permute-start.8 = (bf16[192,512]{1,0:T(8,128)(2,1)S(1)}, bf16[192,512]{1,0:T(8,128)(2,1)S(1)}, u32[]{:S(2)}, u32[]{:S(2)}) collective-permute-start(bf16[192,512]{1,0:T(8,128)(2,1)S(1)} %pad_maximum_fusion), channel_id=1, source_target_pairs={{0,4},{4,0},{8,12},{12,8},{16,20},{20,16},{24,28},{28,24},{32,36},... | collective-permute-start | bytes 589832 | tf_op jit(solution)/shard_map/ppermute | solution.py:529
  28.4 7.5 %collective-permute-start.12 = (bf16[48,256]{1,0:T(8,128)(2,1)S(1)}, bf16[48,256]{1,0:T(8,128)(2,1)S(1)}, u32[]{:S(2)}, u32[]{:S(2)}) collective-permute-start(bf16[48,256]{1,0:T(8,128)(2,1)S(1)} %slice.20), channel_id=1, source_target_pairs={{0,24},{4,28},{8,16},{12,20},{16,8},{20,12},{24,0},{28,4},{32,56},... | collective-permute-start | bytes 73736 | tf_op jit(solution)/shard_map/ppermute | solution.py:529
  32.3 4.2 %collective-permute-start.11 = (bf16[48,256]{1,0:T(8,128)(2,1)S(1)}, bf16[48,256]{1,0:T(8,128)(2,1)S(1)}, u32[]{:S(2)}, u32[]{:S(2)}) collective-permute-start(bf16[48,256]{1,0:T(8,128)(2,1)S(1)} %slice.20), channel_id=1, source_target_pairs={{0,16},{4,20},{8,24},{12,28},{16,0},{20,4},{24,8},{28,12},{32,48},... | collective-permute-start | bytes 73736 | tf_op jit(solution)/shard_map/ppermute | solution.py:529
  32.3 4.2 %collective-permute-start.10 = (bf16[144,256]{1,0:T(8,128)(2,1)S(1)}, bf16[144,256]{1,0:T(8,128)(2,1)S(1)}, u32[]{:S(2)}, u32[]{:S(2)}) collective-permute-start(bf16[144,256]{1,0:T(8,128)(2,1)S(1)} %finish_low.1.g23_ref.own), channel_id=1, source_target_pairs={{0,8},{4,12},{8,0},{12,4},{16,24},{20,28},{24,16},{28,20},{32,40},... | collective-permute-start | bytes 221192 | tf_op jit(solution)/shard_map/ppermute | solution.py:529
  36.5 3.0 %collective-permute-start.13 = (bf16[576,256]{1,0:T(8,128)(2,1)S(1)}, bf16[576,256]{1,0:T(8,128)(2,1)S(1)}, u32[]{:S(2)}, u32[]{:S(2)}) collective-permute-start(bf16[576,256]{1,0:T(8,128)(2,1)S(1)} %constant_dynamic-update-slice_fusion), channel_id=1, source_target_pairs={{0,4},{4,0},{8,12},{12,8},{16,20},{20,16},{24,28},{28,24},{32,36},... | collective-permute-start | bytes 884744 | tf_op jit(solution)/shard_map/ppermute | solution.py:529

commit v3 on v2

--- a/solution.py
+++ b/solution.py
@@ -168,14 +168,16 @@
     n = x.shape[0]
     lane = iota((n, SLOT), 1)
     tiles = [x[:, i * SLOT : (i + 1) * SLOT].astype(F32) for i in range(4)]
-    slots = [jnp.where(lane < HEAD_DIM, t, 0.0) for t in tiles]
+    slots = [jnp.where(lane < HEAD_DIM, t, 0.0) for t in tiles[:2]] + [None, None]
     ones = jnp.where(lane < HEAD_DIM + 2, 1.0, 0.0)
     for a in range(2):
         low = pltpu.roll(tiles[2 * a], SPARE, 1)
         high = pltpu.roll(tiles[2 * a + 1], SLOT - HEAD_DIM + SPARE, 1)
         slots.append(jnp.where(lane < SPARE, low, jnp.where(lane < HEAD_DIM, high, ones)))
+    out[at : at + n, PAIR : 2 * PAIR] = x[:, PAIR:]
     for i, slot in enumerate(slots):
-        out[at : at + n, i * SLOT : (i + 1) * SLOT] = slot.astype(BF16)
+        if slot is not None:
+            out[at : at + n, i * SLOT : (i + 1) * SLOT] = slot.astype(BF16)
 
 
 def places(g, n, place, shape, axis):
@@ -204,7 +206,9 @@
         for i, (ref, at) in enumerate(parts):
             unpack(f_ref.at[g - 1], i * n, ref[at : at + n, :])
         place = lax.rem(info[PLACE], 1 << g)
-        at_key = places(g, n, place, (tok, SLOT), 0)
+        at_key = jnp.concatenate(
+            [iota((n, SLOT), 0) + (place ^ m) * n for m in ORDER[g]], 0
+        )
         at_query = places(g, n, place, (1, tok), 1)
         for b in range(tok // SLOT):
             lo, hi = b * SLOT, (b + 1) * SLOT
@@ -388,7 +392,7 @@
         grads[g, a] = (pqs[g][a].astype(F32) * x).astype(BF16)
     for g, a in chain:
         k = f_ref[g - 1, :, PAIR + a * SLOT : PAIR + (a + 1) * SLOT]
-        place_rows(b_scr.at[a], first[g], g, a, dot(grads[g, a], k, NN) * SCALE)
+        place_rows(b_scr.at[a], first[g], g, a, clear(dot(grads[g, a], k, NN) * SCALE))
     halves = []
     for a in range(2):
         full = dot(spreads[a], b_scr[a], NN)

time: 42.2 us -> 42.1 us (level)
  no operation moved by 1% of the time
where the time goes in v3:
time: 42.1 us; the launch traced here: 42 us
  starting transfers between devices  20.6 us (49%)
  Pallas kernels  15.8 us (38%)
  waiting for transfers between devices  4.41 us (10%)
  between operations  1.01 us (2%)
    pallas_call x10, Pallas kernels, call(): pl.pallas_call(kernel, out_shape=outs, in_specs=specs, out_specs=jax.tree...  15.8 us
    ppermute x10, starting transfers between devices, swap(): return lax.ppermute(x, 'seq', [(i, i ^ mask) for i in range(n_seq)])  14.5 us
    ppermute x1, starting transfers between devices, on_device(): right = lax.ppermute(out_grad, 'head', left_way)  3.38 us
    ppermute x1, starting transfers between devices, on_device(): far2 = lax.ppermute(right[half:], 'head', left_way)  2.66 us
    ppermute x1, waiting for transfers between devices, on_device(): left = lax.ppermute(out_grad, 'head', right_way)  2.65 us
    ppermute x10, waiting for transfers between devices, swap(): return lax.ppermute(x, 'seq', [(i, i ^ mask) for i in range(n_seq)])  1.75 us
  transfers between devices with their start and end apart: 14, of which 3 were waited for; matrix products, arithmetic and copies ran while one was open for 0% of the time, Pallas kernels for 30%

profile of v3, /device:TPU:1, one launch (start us, length us, event | category | flops | bytes accessed | tf_op | source)
XLA Modules:
  0.0 42.0 jit_solution(15728946929531228011)
XLA Ops:
  0.6 3.4 %collective-permute-start.1 = (bf16[384,640]{1,0:T(8,128)(2,1)}, bf16[384,640]{1,0:T(8,128)(2,1)S(1)}, u32[]{:S(2)}, u32[]{:S(2)}) collective-permute-start(bf16[384,640]{1,0:T(8,128)(2,1)} %og_hbm.1), channel_id=1, source_target_pairs={{0,3},{1,0},{2,1},{3,2},{4,7},{5,4},{6,5},{7,6},{8,11},{9,8},{10,9... | collective-permute-start | bytes 1474568 | tf_op jit(solution)/shard_map/ppermute | solution.py:543
  4.1 3.1 %select.7 = (bf16[384,768]{1,0:T(8,128)(2,1)S(1)}, bf16[336,512]{1,0:T(8,128)(2,1)S(1)}, bf16[144,512]{1,0:T(8,128)(2,1)S(1)}, bf16[2,336,384]{2,1,0:T(8,128)(2,...) custom-call(s32[5]{0:T(128)S(1)} %stack.23.info, ...), custom_call_target="tpu_custom_call" | custom-call | tf_op jit(solution)/shard_map/select/pallas_call | solution.py:506
  7.2 1.7 %collective-permute-start.2 = (bf16[144,512]{1,0:T(8,128)(2,1)S(1)}, bf16[144,512]{1,0:T(8,128)(2,1)S(1)}, u32[]{:S(2)}, u32[]{:S(2)}) collective-permute-start(bf16[144,512]{1,0:T(8,128)(2,1)S(1)} %get-tuple-element.44), channel_id=1, source_target_pairs={{0,8},{4,12},{8,0},{12,4},{16,24},{20,28},{24,16},{28,20},{32,40},... | collective-permute-start | bytes 442376 | tf_op jit(solution)/shard_map/ppermute | solution.py:533
  8.9 2.2 %collective-permute-start.4 = (bf16[48,512]{1,0:T(8,128)(2,1)S(1)}, bf16[48,512]{1,0:T(8,128)(2,1)S(1)}, u32[]{:S(2)}, u32[]{:S(2)}) collective-permute-start(bf16[48,512]{1,0:T(8,128)(2,1)S(1)} %slice.15), channel_id=1, source_target_pairs={{0,24},{4,28},{8,16},{12,20},{16,8},{20,12},{24,0},{28,4},{32,56},... | collective-permute-start | bytes 147464 | tf_op jit(solution)/shard_map/ppermute | solution.py:533
  11.2 1.1 %collective-permute-start.3 = (bf16[48,512]{1,0:T(8,128)(2,1)S(1)}, bf16[48,512]{1,0:T(8,128)(2,1)S(1)}, u32[]{:S(2)}, u32[]{:S(2)}) collective-permute-start(bf16[48,512]{1,0:T(8,128)(2,1)S(1)} %slice.15), channel_id=1, source_target_pairs={{0,16},{4,20},{8,24},{12,28},{16,0},{20,4},{24,8},{28,12},{32,48},... | collective-permute-start | bytes 147464 | tf_op jit(solution)/shard_map/ppermute | solution.py:533
  12.3 1.4 %own_forward.1 = (bf16[2,384,384]{2,1,0:T(8,128)(2,1)S(1)}, f32[384,256]{1,0:T(8,128)S(1)}) custom-call(bf16[384,768]{1,0:T(8,128)(2,1)S(1)} %get-tuple-element.37.s0_ref), custom_call_target="tpu_custom_call" | custom-call | tf_op jit(solution)/shard_map/own_forward/pallas_call | solution.py:506
  13.8 0.8 %project_own.1.acc_in = f32[4,384,160]{2,1,0:T(8,128)S(1)} custom-call(bf16[384,640]{1,0:T(8,128)(2,1)S(1)} %get-tuple-element.40.own, bf16[4,640,640]{2,1,0:T(8,128)(2,1)S(1)} %get-tuple-element.41.wt), custom_call_target="tpu_custom_call" | custom-call | tf_op jit(solution)/shard_map/project_own/pallas_call | solution.py:506
  14.6 2.6 %collective-permute-done.left = bf16[384,640]{1,0:T(8,128)(2,1)S(1)} collective-permute-done((bf16[384,640]{1,0:T(8,128)(2,1)}, bf16[384,640]{1,0:T(8,128)(2,1)S(1)}, u32[]{:S(2)}, u32[]{:S(2)}) %collective-permute-start) | collective-permute-done | bytes 491552 | tf_op jit(solution)/shard_map/ppermute | solution.py:542
  17.4 2.7 %collective-permute-start.6 = (bf16[192,640]{1,0:T(8,128)(2,1)S(1)}, bf16[192,640]{1,0:T(8,128)(2,1)S(1)}, u32[]{:S(2)}, u32[]{:S(2)}) collective-permute-start(bf16[192,640]{1,0:T(8,128)(2,1)S(1)} %slice.17), channel_id=1, source_target_pairs={{0,3},{1,0},{2,1},{3,2},{4,7},{5,4},{6,5},{7,6},{8,11},{9,8},{10,9... | collective-permute-start | bytes 737288 | tf_op jit(solution)/shard_map/ppermute | solution.py:587
  20.1 2.5 %collective-permute-start.9 = (bf16[192,512]{1,0:T(8,128)(2,1)S(1)}, bf16[192,512]{1,0:T(8,128)(2,1)S(1)}, u32[]{:S(2)}, u32[]{:S(2)}) collective-permute-start(bf16[192,512]{1,0:T(8,128)(2,1)S(1)} %pad_maximum_fusion.1), channel_id=1, source_target_pairs={{0,4},{4,0},{8,12},{12,8},{16,20},{20,16},{24,28},{28,24},{32,36},... | collective-permute-start | bytes 589832 | tf_op jit(solution)/shard_map/ppermute | solution.py:533
  22.6 0.1 collective-permute-start.7
  22.7 0.4 collective-permute-start.8
  23.1 1.4 %project_near.1.acc = f32[4,384,160]{2,1,0:T(8,128)S(1)} custom-call(f32[4,384,160]{2,1,0:T(8,128)S(1)} %project_own.1.acc_in, bf16[384,640]{1,0:T(8,128)(2,1)S(1)} %collective-permute-done.left, bf16[384,640]{1,0:T(8,128)(2,1)S(1)} %collective-permute-done.1.right, bf16[4,640,640]{2,1,0:T(8,128)(2,1)S(1)} %get-tuple-element.41.wt), custom_call_target="tpu_custom_call" | custom-call | tf_op jit(solution)/shard_map/project_near/pallas_call | solution.py:506
  24.5 2.8 %segment_forward.1 = (bf16[3,384,768]{2,1,0:T(8,128)(2,1)S(1)}, f32[192,256]{1,0:T(8,128)S(1)}, f32[144,256]{1,0:T(8,128)S(1)}, bf16[2,192,384]{2,1,0:T(8,128)(2...) custom-call(s32[5]{0:T(128)S(1)} %stack.23.info, ...), custom_call_target="tpu_custom_call" | custom-call | tf_op jit(solution)/shard_map/segment_forward/pallas_call | solution.py:506
  27.4 0.9 %finish_low.1.g23_ref.own = bf16[144,256]{1,0:T(8,128)(2,1)S(1)} custom-call(bf16[2,336,384]{2,1,0:T(8,128)(2,1)S(1)} %get-tuple-element.39.picks, f32[4,384,160]{2,1,0:T(8,128)S(1)} %project_near.1.acc, bf16[192,640]{1,0:T(8,128)(2,1)S(1)} %collective-permute-done.5.far1, bf16[192,640]{1,0:T(8,128)(2,1)S(1)} %collective-permute-done.6.far2, ...), custom_call_target="tpu_custom_call" | custom-call | tf_op jit(solution)/shard_map/finish_low/pallas_call | solution.py:506
  28.3 3.8 %collective-permute-start.12 = (bf16[48,256]{1,0:T(8,128)(2,1)S(1)}, bf16[48,256]{1,0:T(8,128)(2,1)S(1)}, u32[]{:S(2)}, u32[]{:S(2)}) collective-permute-start(bf16[48,256]{1,0:T(8,128)(2,1)S(1)} %slice.20), channel_id=1, source_target_pairs={{0,24},{4,28},{8,16},{12,20},{16,8},{20,12},{24,0},{28,4},{32,56},... | collective-permute-start | bytes 73736 | tf_op jit(solution)/shard_map/ppermute | solution.py:533
  32.1 0.7 %collective-permute-start.10 = (bf16[144,256]{1,0:T(8,128)(2,1)S(1)}, bf16[144,256]{1,0:T(8,128)(2,1)S(1)}, u32[]{:S(2)}, u32[]{:S(2)}) collective-permute-start(bf16[144,256]{1,0:T(8,128)(2,1)S(1)} %finish_low.1.g23_ref.own), channel_id=1, source_target_pairs={{0,8},{4,12},{8,0},{12,4},{16,24},{20,28},{24,16},{28,20},{32,40},... | collective-permute-start | bytes 221192 | tf_op jit(solution)/shard_map/ppermute | solution.py:533
  32.8 0.9 %finish_high.1 = (bf16[384,256]{1,0:T(8,128)(2,1)S(1)}, bf16[192,256]{1,0:T(8,128)(2,1)S(1)}) custom-call(bf16[2,336,384]{2,1,0:T(8,128)(2,1)S(1)} %get-tuple-element.39.picks, f32[4,384,160]{2,1,0:T(8,128)S(1)} %project_near.1.acc, bf16[192,640]{1,0:T(8,128)(2,1)S(1)} %collective-permute-done.5.far1, bf16[192,640]{1,0:T(8,128)(2,1)S(1)} %collective-permute-done.6.far2, ...), custom_call_target="tpu_custom_call" | custom-call | tf_op jit(solution)/shard_map/finish_high/pallas_call | solution.py:506
  33.8 0.9 %own_backward.1.d_ref = bf16[384,768]{1,0:T(8,128)(2,1)S(1)} custom-call(bf16[384,768]{1,0:T(8,128)(2,1)S(1)} %get-tuple-element.37.s0_ref, bf16[2,384,384]{2,1,0:T(8,128)(2,1)S(1)} %get-tuple-element.38.p_ref, bf16[384,256]{1,0:T(8,128)(2,1)S(1)} %get-tuple-element.56.g_ref), custom_call_target="tpu_custom_call" | custom-call | tf_op jit(solution)/shard_map/own_backward/pallas_call | solution.py:506
  34.7 1.1 %query_side.1.query_in = bf16[384,640]{1,0:T(8,128)(2,1)S(1)} custom-call(bf16[2,384,336]{2,1,0:T(8,128)(2,1)S(1)} %get-tuple-element.36.spreads, bf16[384,768]{1,0:T(8,128)(2,1)S(1)} %own_backward.1.d_ref, bf16[3,384,768]{2,1,0:T(8,128)(2,1)S(1)} %get-tuple-element.57.f_ref, bf16[192,256]{1,0:T(8,128)(2,1)S(1)} %get-tuple-element.58.g1_ref.own1, ...), custom_call_target="tpu_custom_call" | custom-call | tf_op jit(solution)/shard_map/query_side/pallas_call | solution.py:506
  35.8 0.5 %collective-permute-done.11.r4 = bf16[48,256]{1,0:T(8,128)(2,1)S(1)} collective-permute-done((bf16[48,256]{1,0:T(8,128)(2,1)S(1)}, bf16[48,256]{1,0:T(8,128)(2,1)S(1)}, u32[]{:S(2)}, u32[]{:S(2)}) %collective-permute-start.11) | collective-permute-done | bytes 24608 | tf_op jit(solution)/shard_map/ppermute | solution.py:533
  36.3 1.8 %collective-permute-start.13 = (bf16[576,256]{1,0:T(8,128)(2,1)S(1)}, bf16[576,256]{1,0:T(8,128)(2,1)S(1)}, u32[]{:S(2)}, u32[]{:S(2)}) collective-permute-start(bf16[576,256]{1,0:T(8,128)(2,1)S(1)} %constant_dynamic-update-slice_fusion), channel_id=1, source_target_pairs={{0,4},{4,0},{8,12},{12,8},{16,20},{20,16},{24,28},{28,24},{32,36},... | collective-permute-start | bytes 884744 | tf_op jit(solution)/shard_map/ppermute | solution.py:533
  38.2 1.2 %collective-permute-done.13.d = bf16[576,256]{1,0:T(8,128)(2,1)S(1)} collective-permute-done((bf16[576,256]{1,0:T(8,128)(2,1)S(1)}, bf16[576,256]{1,0:T(8,128)(2,1)S(1)}, u32[]{:S(2)}, u32[]{:S(2)}) %collective-permute-start.13) | collective-permute-done | bytes 294944 | tf_op jit(solution)/shard_map/ppermute | solution.py:533
  39.4 2.4 %key_value.1 = (bf16[384,640]{1,0:T(8,128)(2,1)}, bf16[384,640]{1,0:T(8,128)(2,1)}, bf16[384,640]{1,0:T(8,128)(2,1)}) custom-call(bf16[2,384,336]{2,1,0:T(8,128)(2,1)S(1)} %get-tuple-element.36.spreads, bf16[384,640]{1,0:T(8,128)(2,1)S(1)} %query_side.1.query_in, bf16[384,768]{1,0:T(8,128)(2,1)S(1)} %own_backward.1.d_ref, ...), custom_call_target="tpu_custom_call" | custom-call | tf_op jit(solution)/shard_map/key_value/pallas_call | solution.py:506
  (27 shorter events, 0.3 us)
Async XLA Ops:
  0.6 13.9 %collective-permute-start.1 = (bf16[384,640]{1,0:T(8,128)(2,1)}, bf16[384,640]{1,0:T(8,128)(2,1)S(1)}, u32[]{:S(2)}, u32[]{:S(2)}) collective-permute-start(bf16[384,640]{1,0:T(8,128)(2,1)} %og_hbm.1), channel_id=1, source_target_pairs={{0,3},{1,0},{2,1},{3,2},{4,7},{5,4},{6,5},{7,6},{8,11},{9,8},{10,9... | collective-permute-start | bytes 1474568 | tf_op jit(solution)/shard_map/ppermute | solution.py:543
  4.0 13.2 %collective-permute-start = (bf16[384,640]{1,0:T(8,128)(2,1)}, bf16[384,640]{1,0:T(8,128)(2,1)S(1)}, u32[]{:S(2)}, u32[]{:S(2)}) collective-permute-start(bf16[384,640]{1,0:T(8,128)(2,1)} %og_hbm.1), channel_id=1, source_target_pairs={{0,1},{1,2},{2,3},{3,0},{4,5},{5,6},{6,7},{7,4},{8,9},{9,10},{10,1... | collective-permute-start | bytes 1474568 | tf_op jit(solution)/shard_map/ppermute | solution.py:542
  7.2 10.0 %collective-permute-start.2 = (bf16[144,512]{1,0:T(8,128)(2,1)S(1)}, bf16[144,512]{1,0:T(8,128)(2,1)S(1)}, u32[]{:S(2)}, u32[]{:S(2)}) collective-permute-start(bf16[144,512]{1,0:T(8,128)(2,1)S(1)} %get-tuple-element.44), channel_id=1, source_target_pairs={{0,8},{4,12},{8,0},{12,4},{16,24},{20,28},{24,16},{28,20},{32,40},... | collective-permute-start | bytes 442376 | tf_op jit(solution)/shard_map/ppermute | solution.py:533
  8.9 8.3 %collective-permute-start.4 = (bf16[48,512]{1,0:T(8,128)(2,1)S(1)}, bf16[48,512]{1,0:T(8,128)(2,1)S(1)}, u32[]{:S(2)}, u32[]{:S(2)}) collective-permute-start(bf16[48,512]{1,0:T(8,128)(2,1)S(1)} %slice.15), channel_id=1, source_target_pairs={{0,24},{4,28},{8,16},{12,20},{16,8},{20,12},{24,0},{28,4},{32,56},... | collective-permute-start | bytes 147464 | tf_op jit(solution)/shard_map/ppermute | solution.py:533
  11.2 6.0 %collective-permute-start.3 = (bf16[48,512]{1,0:T(8,128)(2,1)S(1)}, bf16[48,512]{1,0:T(8,128)(2,1)S(1)}, u32[]{:S(2)}, u32[]{:S(2)}) collective-permute-start(bf16[48,512]{1,0:T(8,128)(2,1)S(1)} %slice.15), channel_id=1, source_target_pairs={{0,16},{4,20},{8,24},{12,28},{16,0},{20,4},{24,8},{28,12},{32,48},... | collective-permute-start | bytes 147464 | tf_op jit(solution)/shard_map/ppermute | solution.py:533
  17.3 10.0 %collective-permute-start.5 = (bf16[192,640]{1,0:T(8,128)(2,1)S(1)}, bf16[192,640]{1,0:T(8,128)(2,1)S(1)}, u32[]{:S(2)}, u32[]{:S(2)}) collective-permute-start(bf16[192,640]{1,0:T(8,128)(2,1)S(1)} %slice.16), channel_id=1, source_target_pairs={{0,1},{1,2},{2,3},{3,0},{4,5},{5,6},{6,7},{7,4},{8,9},{9,10},{10,1... | collective-permute-start | bytes 737288 | tf_op jit(solution)/shard_map/ppermute | solution.py:586
  17.4 10.0 %collective-permute-start.6 = (bf16[192,640]{1,0:T(8,128)(2,1)S(1)}, bf16[192,640]{1,0:T(8,128)(2,1)S(1)}, u32[]{:S(2)}, u32[]{:S(2)}) collective-permute-start(bf16[192,640]{1,0:T(8,128)(2,1)S(1)} %slice.17), channel_id=1, source_target_pairs={{0,3},{1,0},{2,1},{3,2},{4,7},{5,4},{6,5},{7,6},{8,11},{9,8},{10,9... | collective-permute-start | bytes 737288 | tf_op jit(solution)/shard_map/ppermute | solution.py:587
  20.1 4.4 %collective-permute-start.9 = (bf16[192,512]{1,0:T(8,128)(2,1)S(1)}, bf16[192,512]{1,0:T(8,128)(2,1)S(1)}, u32[]{:S(2)}, u32[]{:S(2)}) collective-permute-start(bf16[192,512]{1,0:T(8,128)(2,1)S(1)} %pad_maximum_fusion.1), channel_id=1, source_target_pairs={{0,4},{4,0},{8,12},{12,8},{16,20},{20,16},{24,28},{28,24},{32,36},... | collective-permute-start | bytes 589832 | tf_op jit(solution)/shard_map/ppermute | solution.py:533
  22.6 1.9 %collective-permute-start.7 = (bf16[192,512]{1,0:T(8,128)(2,1)S(1)}, bf16[192,512]{1,0:T(8,128)(2,1)S(1)}, u32[]{:S(2)}, u32[]{:S(2)}) collective-permute-start(bf16[192,512]{1,0:T(8,128)(2,1)S(1)} %slice.18), channel_id=1, source_target_pairs={{0,4},{4,0},{8,12},{12,8},{16,20},{20,16},{24,28},{28,24},{32,36},... | collective-permute-start | bytes 589832 | tf_op jit(solution)/shard_map/ppermute | solution.py:533
  22.7 1.8 %collective-permute-start.8 = (bf16[192,512]{1,0:T(8,128)(2,1)S(1)}, bf16[192,512]{1,0:T(8,128)(2,1)S(1)}, u32[]{:S(2)}, u32[]{:S(2)}) collective-permute-start(bf16[192,512]{1,0:T(8,128)(2,1)S(1)} %pad_maximum_fusion), channel_id=1, source_target_pairs={{0,4},{4,0},{8,12},{12,8},{16,20},{20,16},{24,28},{28,24},{32,36},... | collective-permute-start | bytes 589832 | tf_op jit(solution)/shard_map/ppermute | solution.py:533
  28.3 7.5 %collective-permute-start.12 = (bf16[48,256]{1,0:T(8,128)(2,1)S(1)}, bf16[48,256]{1,0:T(8,128)(2,1)S(1)}, u32[]{:S(2)}, u32[]{:S(2)}) collective-permute-start(bf16[48,256]{1,0:T(8,128)(2,1)S(1)} %slice.20), channel_id=1, source_target_pairs={{0,24},{4,28},{8,16},{12,20},{16,8},{20,12},{24,0},{28,4},{32,56},... | collective-permute-start | bytes 73736 | tf_op jit(solution)/shard_map/ppermute | solution.py:533
  32.1 4.2 %collective-permute-start.11 = (bf16[48,256]{1,0:T(8,128)(2,1)S(1)}, bf16[48,256]{1,0:T(8,128)(2,1)S(1)}, u32[]{:S(2)}, u32[]{:S(2)}) collective-permute-start(bf16[48,256]{1,0:T(8,128)(2,1)S(1)} %slice.20), channel_id=1, source_target_pairs={{0,16},{4,20},{8,24},{12,28},{16,0},{20,4},{24,8},{28,12},{32,48},... | collective-permute-start | bytes 73736 | tf_op jit(solution)/shard_map/ppermute | solution.py:533
  32.1 4.2 %collective-permute-start.10 = (bf16[144,256]{1,0:T(8,128)(2,1)S(1)}, bf16[144,256]{1,0:T(8,128)(2,1)S(1)}, u32[]{:S(2)}, u32[]{:S(2)}) collective-permute-start(bf16[144,256]{1,0:T(8,128)(2,1)S(1)} %finish_low.1.g23_ref.own), channel_id=1, source_target_pairs={{0,8},{4,12},{8,0},{12,4},{16,24},{20,28},{24,16},{28,20},{32,40},... | collective-permute-start | bytes 221192 | tf_op jit(solution)/shard_map/ppermute | solution.py:533
  36.3 3.0 %collective-permute-start.13 = (bf16[576,256]{1,0:T(8,128)(2,1)S(1)}, bf16[576,256]{1,0:T(8,128)(2,1)S(1)}, u32[]{:S(2)}, u32[]{:S(2)}) collective-permute-start(bf16[576,256]{1,0:T(8,128)(2,1)S(1)} %constant_dynamic-update-slice_fusion), channel_id=1, source_target_pairs={{0,4},{4,0},{8,12},{12,8},{16,20},{20,16},{24,28},{28,24},{32,36},... | collective-permute-start | bytes 884744 | tf_op jit(solution)/shard_map/ppermute | solution.py:533
